TPU v7x, 32 devices: a whole 2x2x4 slice. The times are simulated.
32 devices in a mesh: dp: 8 (over z, x), tensor: 4 (over y, core).
Axes of the slice: x: 2, y: 2, z: 4, core: 2. Of those that a mesh axis runs over, the one named last changes fastest.
Arguments:
- tokens: bfloat16 [16384, 768], P(('dp', 'tensor')), may hold values from -6 to 6
- segment: int32 [16384], P(('dp', 'tensor')), may hold values from 0 to 512, as said below
- live: int32 [16384], P(('dp', 'tensor')), may hold values from 0 to 1, as said below
- mix_weight: bfloat16 [3, 768, 768], replicated, may hold values from -0.21875 to 0.21875
- out_weight: bfloat16 [768, 768], replicated, may hold values from -0.875 to 0.875
- position_table: bfloat16 [512, 768], replicated, may hold values from -6 to 6
- norm_gain: float32 [2, 768], replicated, may hold values from 0.5 to 1.5
- norm_bias: float32 [2, 768], replicated, may hold values from -1.5 to 1.5
- mix_left: bfloat16 [4, 768, 12], replicated, may hold values from -0.21875 to 0.21875
- mix_scale: float32 [4, 12], replicated, may hold values from -3 to 3
- mix_right: bfloat16 [4, 12, 768], replicated, may hold values from -1.75 to 1.75
- expand_weight: bfloat16 [768, 3072], P(None, 'tensor'), may hold values from -0.21875 to 0.21875
- expand_left: bfloat16 [768, 12], replicated, may hold values from -0.21875 to 0.21875
- expand_right: bfloat16 [12, 3072], P(None, 'tensor'), may hold values from -1.75 to 1.75
- shrink_weight: bfloat16 [3072, 768], P('tensor'), may hold values from -0.21875 to 0.21875
- shrink_left: bfloat16 [3072, 12], P('tensor'), may hold values from -0.21875 to 0.21875
- feed_scale: float32 [2, 12], replicated, may hold values from -3 to 3
- shrink_right: bfloat16 [12, 768], replicated, may hold values from -1.75 to 1.75
- cotangent: bfloat16 [16384, 768], P(('dp', 'tensor'))
Outputs:
- layer_out: bfloat16 [16384, 768], P(('dp', 'tensor'))
- grad_tokens: float32 [16384, 768], P(('dp', 'tensor'))
- grad_mix_left: float32 [4, 768, 12], replicated
- grad_mix_scale: float32 [4, 12], replicated
- grad_mix_right: float32 [4, 12, 768], replicated
- grad_expand_left: float32 [768, 12], replicated
- grad_expand_right: float32 [12, 3072], P(None, 'tensor')
- grad_shrink_left: float32 [3072, 12], P('tensor')
- grad_feed_scale: float32 [2, 12], replicated
- grad_shrink_right: float32 [12, 768], replicated
Inputs may be any that keep to these rules, and one draw needn't show every extreme that they name: `segment`: within each aligned block of 512 slots (one device's slots) the live slots come first and their sequence numbers start at 0 and never fall; padding slots carry 512; some block holds a single sequence of 512 tokens. In each aligned block of 512 slots the live ones come first, at least 256 of them; some block is fully live.
All inputs are finite; a program needn't handle non-finite values.
Results may differ from a plain program's by a relative error of at most 0.023.
Values may be sent and summed in bfloat16 or wider, within the bound.
A program may use at most 192 MiB of HBM per device.

v0:
```python
import math

import jax
import jax.numpy as jnp
from jax import lax
from jax.sharding import PartitionSpec as P

HEADS = 12
HEAD_DIM = 64
SPAN = 256


norm_eps = 1e-07
masked_fill = -1e30
inverse_root_two = 1.0 / math.sqrt(2.0)
inverse_root_tau = 1.0 / math.sqrt(2.0 * math.pi)


def product(left, right):
    return jnp.dot(left, right, preferred_element_type=jnp.float32)


def product_lead(left, right):
    return lax.dot_general(
        left, right, (((0,), (0,)), ((), ())), preferred_element_type=jnp.float32
    )


def product_trail(left, right):
    return lax.dot_general(
        left, right, (((1,), (1,)), ((), ())), preferred_element_type=jnp.float32
    )


def adapter_forward(inputs, weight, left_factor, scale_vector, right_factor):
    rank_values = product(inputs, left_factor)
    rank_low = (rank_values * scale_vector).astype(jnp.bfloat16)
    return (product(inputs, weight) + product(rank_low, right_factor), rank_values, rank_low)


def adapter_backward(
    grad_out,
    inputs,
    weight,
    left_factor,
    scale_vector,
    right_factor,
    rank_values,
    rank_low,
    need_input,
):
    grad_rank = product_trail(grad_out, right_factor)
    grad_small = (grad_rank * scale_vector).astype(jnp.bfloat16)
    grad_input = None
    if need_input:
        grad_input = product_trail(grad_out, weight) + product_trail(grad_small, left_factor)
    grad_left = product_lead(inputs, grad_small)
    grad_scale = jnp.sum(rank_values * grad_rank, axis=0)
    grad_right = product_lead(rank_low, grad_out)
    return (grad_input, grad_left, grad_scale, grad_right)


def norm_forward(values, gain, shift):
    center = values - jnp.mean(values, axis=-1, keepdims=True)
    root_inverse = lax.rsqrt(jnp.mean(center * center, axis=-1, keepdims=True) + norm_eps)
    unit_rows = center * root_inverse
    return (unit_rows * gain + shift, unit_rows, root_inverse)


def norm_backward(incoming, unit_rows, root_inverse, gain):
    scaled = incoming * gain
    return root_inverse * (
        scaled
        - jnp.mean(scaled, axis=-1, keepdims=True)
        - unit_rows * jnp.mean(scaled * unit_rows, axis=-1, keepdims=True)
    )


def gelu_slope(values):
    return (
        0.5 * (1.0 + lax.erf(values * inverse_root_two))
        + values * jnp.exp(-0.5 * values * values) * inverse_root_tau
    )


def heads_first(values):
    return jnp.transpose(values.reshape(values.shape[0], HEADS, HEAD_DIM), (1, 0, 2))


def heads_merged(values):
    return jnp.transpose(values, (1, 0, 2)).reshape(values.shape[1], HEADS * HEAD_DIM)


def skew_sizes(length):
    shift = length - SPAN
    lower = max(0, shift)
    upper = min(2 * length, shift + 2 * SPAN)
    first_col = max(0, -shift)
    padding = -2 * length % 128
    return (lower, upper, first_col, padding)


def relative_pick(table_rev):
    groups = table_rev.shape[0]
    length = table_rev.shape[1]
    lower, upper, first_col, padding = skew_sizes(length)
    pieces = [jnp.zeros((groups, length, 1), table_rev.dtype)]
    pieces.append(jnp.broadcast_to(table_rev[:, :, :1], (groups, length, lower)))
    pieces.append(table_rev)
    pieces.append(jnp.broadcast_to(table_rev[:, :, -1:], (groups, length, 2 * length - upper)))
    spread_rows = jnp.concatenate(pieces, axis=2)
    width = spread_rows.shape[2]
    flat_rows = spread_rows.reshape(groups, length * width)[:, : length * (width - 1)]
    return flat_rows.reshape(groups, length, width - 1)[:, :, length : 2 * length]


def relative_fold(grads):
    groups = grads.shape[0]
    length = grads.shape[1]
    lower, upper, first_col, padding = skew_sizes(length)
    width = 2 * length + padding + 1
    placed = jnp.pad(grads, ((0, 0), (0, 0), (length, padding)))
    flat_rows = jnp.pad(placed.reshape(groups, length * (width - 1)), ((0, 0), (0, length)))
    spread_rows = flat_rows.reshape(groups, length, width)[:, :, 1 : 1 + 2 * length].astype(
        jnp.float32
    )
    middle = spread_rows[:, :, lower:upper]
    folded = middle
    lower_sum = jnp.sum(spread_rows[:, :, :lower], axis=2, keepdims=True)
    folded = folded + jnp.pad(lower_sum, ((0, 0), (0, 0), (0, 2 * SPAN - 1)))
    upper_sum = jnp.sum(spread_rows[:, :, upper:], axis=2, keepdims=True)
    folded = folded + jnp.pad(upper_sum, ((0, 0), (0, 0), (2 * SPAN - 1, 0)))
    return folded


def raw_logits(query_per_head, key_per_head, reversed_query_table, reversed_key_table, allowed):
    content = jnp.einsum(
        "hid,hjd->hij", query_per_head, key_per_head, preferred_element_type=jnp.float32
    )
    query_side = jnp.einsum(
        "gan,gfn->gaf", query_per_head, reversed_key_table, preferred_element_type=jnp.float32
    )
    key_side = jnp.einsum(
        "yuq,ykq->yuk", key_per_head, reversed_query_table, preferred_element_type=jnp.float32
    )
    along = relative_pick(query_side)
    across = jnp.swapaxes(relative_pick(key_side), 1, 2)
    logits = (content + along + across) * (1.0 / math.sqrt(3.0 * HEAD_DIM))
    return jnp.where(allowed[None], logits, masked_fill)


def attention_forward(
    query_per_head, key_per_head, head_values, reversed_query_table, reversed_key_table, allowed
):
    logits = raw_logits(
        query_per_head, key_per_head, reversed_query_table, reversed_key_table, allowed
    )
    peaks = jnp.max(logits, axis=-1, keepdims=True)
    weights = jnp.exp(logits - peaks)
    totals = jnp.sum(weights, axis=-1, keepdims=True)
    shares_low = (weights / totals).astype(jnp.bfloat16)
    context = jnp.einsum(
        "hij,hjd->hid", shares_low, head_values, preferred_element_type=jnp.float32
    )
    return (heads_merged(context.astype(jnp.bfloat16)), peaks + jnp.log(totals))


def attention_backward(
    grad_context,
    query_per_head,
    key_per_head,
    head_values,
    reversed_query_table,
    reversed_key_table,
    allowed,
    log_totals,
):
    score_scale = 1.0 / math.sqrt(3.0 * HEAD_DIM)
    logits = raw_logits(
        query_per_head, key_per_head, reversed_query_table, reversed_key_table, allowed
    )
    shares = jnp.exp(logits - log_totals)
    shares_low = shares.astype(jnp.bfloat16)
    grad_heads = heads_first(grad_context)
    grad_shares = jnp.einsum(
        "hid,hjd->hij", grad_heads, head_values, preferred_element_type=jnp.float32
    )
    grad_values = jnp.einsum(
        "hij,hid->hjd", shares_low, grad_heads, preferred_element_type=jnp.float32
    )
    inner_sum = jnp.sum(grad_shares * shares, axis=-1, keepdims=True)
    grad_logits = (shares * (grad_shares - inner_sum)).astype(jnp.bfloat16)
    query_branch_gradient = (relative_fold(grad_logits) * score_scale).astype(jnp.bfloat16)
    key_branch_gradient = (relative_fold(jnp.swapaxes(grad_logits, 1, 2)) * score_scale).astype(
        jnp.bfloat16
    )
    grad_queries = score_scale * jnp.einsum(
        "hij,hjd->hid", grad_logits, key_per_head, preferred_element_type=jnp.float32
    ) + jnp.einsum(
        "bon,bnv->bov",
        query_branch_gradient,
        reversed_key_table,
        preferred_element_type=jnp.float32,
    )
    grad_keys = score_scale * jnp.einsum(
        "hij,hid->hjd", grad_logits, query_per_head, preferred_element_type=jnp.float32
    ) + jnp.einsum(
        "ktc,kcg->ktg",
        key_branch_gradient,
        reversed_query_table,
        preferred_element_type=jnp.float32,
    )
    grad_table_keys = jnp.einsum(
        "onj,onx->ojx", query_branch_gradient, query_per_head, preferred_element_type=jnp.float32
    )
    grad_table_queries = jnp.einsum(
        "ngb,nga->nba", key_branch_gradient, key_per_head, preferred_element_type=jnp.float32
    )
    return (
        heads_merged(grad_queries.astype(jnp.bfloat16)),
        heads_merged(grad_keys.astype(jnp.bfloat16)),
        heads_merged(grad_values.astype(jnp.bfloat16)),
        heads_merged(grad_table_queries.astype(jnp.bfloat16))[::-1],
        heads_merged(grad_table_keys.astype(jnp.bfloat16))[::-1],
    )


def body(
    tokens,
    segment,
    live,
    mix_weight,
    out_weight,
    position_table,
    norm_gain,
    norm_bias,
    mix_left,
    mix_scale,
    mix_right,
    expand_weight,
    expand_left,
    expand_right,
    shrink_weight,
    shrink_left,
    feed_scale,
    shrink_right,
    cotangent,
):
    row_count = tokens.shape[0]
    places = jnp.arange(row_count, dtype=jnp.int32)
    allowed = (segment[:, None] == segment[None, :]) & (
        (live[None, :] == 1) | (places[:, None] == places[None, :])
    )
    projected = [
        adapter_forward(
            tokens, mix_weight[which], mix_left[which], mix_scale[which], mix_right[which]
        )
        for which in range(3)
    ]
    pos_query_parts = adapter_forward(
        position_table, mix_weight[0], mix_left[0], mix_scale[0], mix_right[0]
    )
    pos_key_parts = adapter_forward(
        position_table, mix_weight[1], mix_left[1], mix_scale[1], mix_right[1]
    )
    query_per_head = heads_first(projected[0][0].astype(jnp.bfloat16))
    key_per_head = heads_first(projected[1][0].astype(jnp.bfloat16))
    head_values = heads_first(projected[2][0].astype(jnp.bfloat16))
    reversed_query_table = heads_first(pos_query_parts[0].astype(jnp.bfloat16)[::-1])
    reversed_key_table = heads_first(pos_key_parts[0].astype(jnp.bfloat16)[::-1])
    context, log_totals = attention_forward(
        query_per_head, key_per_head, head_values, reversed_query_table, reversed_key_table, allowed
    )
    attended, out_values, out_low = adapter_forward(
        context, out_weight, mix_left[3], mix_scale[3], mix_right[3]
    )
    normed, leading_unit_vector, root_first = norm_forward(
        tokens.astype(jnp.float32) + attended, norm_gain[0], norm_bias[0]
    )
    hidden = normed.astype(jnp.bfloat16)
    expand_values = product(hidden, expand_left)
    expand_low = (expand_values * feed_scale[0]).astype(jnp.bfloat16)
    rows_all, expand_low_all = (
        lax.all_gather(hidden, "tensor", axis=0, tiled=True),
        lax.all_gather(expand_low, "tensor", axis=0, tiled=True),
    )
    pre_act = product(rows_all, expand_weight) + product(expand_low_all, expand_right)
    active = jax.nn.gelu(pre_act, approximate=False).astype(jnp.bfloat16)
    branch_part, shrink_values = (
        lax.psum_scatter(
            product(active, shrink_weight).astype(jnp.bfloat16),
            "tensor",
            scatter_dimension=0,
            tiled=True,
        ).astype(jnp.float32),
        lax.psum_scatter(
            product(active, shrink_left).astype(jnp.bfloat16),
            "tensor",
            scatter_dimension=0,
            tiled=True,
        ).astype(jnp.float32),
    )
    shrink_low = (shrink_values * feed_scale[1]).astype(jnp.bfloat16)
    branch = branch_part + product(shrink_low, shrink_right)
    layer_out, unit_second, root_second = norm_forward(normed + branch, norm_gain[1], norm_bias[1])
    grad_second = norm_backward(
        cotangent.astype(jnp.float32), unit_second, root_second, norm_gain[1]
    )
    grad_branch = grad_second.astype(jnp.bfloat16)
    grad_shrink_rank = product_trail(grad_branch, shrink_right)
    grad_shrink_small = (grad_shrink_rank * feed_scale[1]).astype(jnp.bfloat16)
    local_shrink_right = product_lead(shrink_low, grad_branch)
    local_shrink_scale = jnp.sum(shrink_values * grad_shrink_rank, axis=0)
    branch_all, shrink_rank_gathered = (
        lax.all_gather(grad_branch, "tensor", axis=0, tiled=True),
        lax.all_gather(grad_shrink_small, "tensor", axis=0, tiled=True),
    )
    grad_active = product_trail(branch_all, shrink_weight) + product_trail(
        shrink_rank_gathered, shrink_left
    )
    local_shrink_left = product_lead(active, shrink_rank_gathered)
    grad_pre = (grad_active * gelu_slope(pre_act)).astype(jnp.bfloat16)
    local_expand_right = product_lead(expand_low_all, grad_pre)
    grad_rows, grad_expand_rank = (
        lax.psum_scatter(
            product_trail(grad_pre, expand_weight), "tensor", scatter_dimension=0, tiled=True
        ),
        lax.psum_scatter(
            product_trail(grad_pre, expand_right), "tensor", scatter_dimension=0, tiled=True
        ),
    )
    grad_expand_small = (grad_expand_rank * feed_scale[0]).astype(jnp.bfloat16)
    grad_hidden = grad_rows + product_trail(grad_expand_small, expand_left)
    local_expand_left = product_lead(hidden, grad_expand_small)
    local_expand_scale = jnp.sum(expand_values * grad_expand_rank, axis=0)
    grad_first = norm_backward(
        grad_second + grad_hidden, leading_unit_vector, root_first, norm_gain[0]
    )
    grad_attended = grad_first.astype(jnp.bfloat16)
    grad_context_full, out_left, out_scale, out_right = adapter_backward(
        grad_attended,
        context,
        out_weight,
        mix_left[3],
        mix_scale[3],
        mix_right[3],
        out_values,
        out_low,
        True,
    )
    grad_queries, grad_keys, grad_values, grad_table_queries, grad_table_keys = attention_backward(
        grad_context_full.astype(jnp.bfloat16),
        query_per_head,
        key_per_head,
        head_values,
        reversed_query_table,
        reversed_key_table,
        allowed,
        log_totals,
    )
    incoming = (grad_queries, grad_keys, grad_values)
    token_parts = [
        adapter_backward(
            incoming[which],
            tokens,
            mix_weight[which],
            mix_left[which],
            mix_scale[which],
            mix_right[which],
            projected[which][1],
            projected[which][2],
            True,
        )
        for which in range(3)
    ]
    query_table = adapter_backward(
        grad_table_queries,
        position_table,
        mix_weight[0],
        mix_left[0],
        mix_scale[0],
        mix_right[0],
        pos_query_parts[1],
        pos_query_parts[2],
        False,
    )
    key_table = adapter_backward(
        grad_table_keys,
        position_table,
        mix_weight[1],
        mix_left[1],
        mix_scale[1],
        mix_right[1],
        pos_key_parts[1],
        pos_key_parts[2],
        False,
    )
    grad_tokens = grad_first + token_parts[0][0] + token_parts[1][0] + token_parts[2][0]
    local_left = jnp.stack(
        [
            token_parts[0][1] + query_table[1],
            token_parts[1][1] + key_table[1],
            token_parts[2][1],
            out_left,
        ]
    )
    local_scale = jnp.stack(
        [
            token_parts[0][2] + query_table[2],
            token_parts[1][2] + key_table[2],
            token_parts[2][2],
            out_scale,
        ]
    )
    local_right = jnp.stack(
        [
            token_parts[0][3] + query_table[3],
            token_parts[1][3] + key_table[3],
            token_parts[2][3],
            out_right,
        ]
    )
    local_feed = jnp.stack([local_expand_scale, local_shrink_scale])
    summed = lax.psum(
        (local_left, local_scale, local_right, local_expand_left, local_feed, local_shrink_right),
        ("dp", "tensor"),
    )
    split_sums = (
        lax.psum(local_expand_right.astype(jnp.bfloat16), "dp").astype(jnp.float32),
        lax.psum(local_shrink_left.astype(jnp.bfloat16), "dp").astype(jnp.float32),
    )
    expand_right_grad = split_sums[0]
    shrink_left_grad = split_sums[1]
    return (
        layer_out.astype(jnp.bfloat16),
        grad_tokens,
        summed[0],
        summed[1],
        summed[2],
        summed[3],
        expand_right_grad,
        shrink_left_grad,
        summed[4],
        summed[5],
    )


def solution(mesh):
    return jax.shard_map(
        body,
        mesh=mesh,
        in_specs=(
            P(("dp", "tensor"), None),
            P(("dp", "tensor")),
            P(("dp", "tensor")),
            P(),
            P(),
            P(),
            P(),
            P(),
            P(),
            P(),
            P(),
            P(None, "tensor"),
            P(),
            P(None, "tensor"),
            P("tensor", None),
            P("tensor", None),
            P(),
            P(),
            P(("dp", "tensor"), None),
        ),
        out_specs=(
            P(("dp", "tensor"), None),
            P(("dp", "tensor"), None),
            P(),
            P(),
            P(),
            P(),
            P(None, "tensor"),
            P("tensor", None),
            P(),
            P(),
        ),
        check_vma=False,
    )
```

profile of v0, /device:TPU:0, one launch (start us, length us, event | category | flops | bytes accessed | tf_op | source)
XLA Modules:
  0.0 1476.3 jit_solution(15260422768311068677)
XLA Ops:
  39.5 77.9 %concatenate.8 = f32[12,512,1025]{1,2,0:T(8,128)} concatenate(f32[12,512,1]{1,2,0:T(1,128)S(1)} %broadcast.143, f32[12,512,256]{1,2,0:T(8,128)} %broadcast_in_dim.42, f32[12,512,512]{1,2,0:T(8,128)} %copy-done.4, f32[12,512,256]{1,2,0:T(8,128)} %broadcast_in_dim.44), dimensions={2} | concatenate | bytes 50380800 | tf_op jit(solution)/shard_map/concatenate | solution.py:111
  117.4 25.9 %copy.52 = f32[12,512,1025]{2,1,0:T(8,128)} copy(f32[12,512,1025]{1,2,0:T(8,128)} %concatenate.8) | data formatting | bytes 50380800 | tf_op jit(solution)/shard_map/concatenate | solution.py:111
  143.3 41.1 %reshape.219 = f32[12,524800]{1,0:T(8,128)} reshape(f32[12,512,1025]{2,1,0:T(8,128)} %copy.52) | data formatting | bytes 50380800 | tf_op jit(solution)/shard_map/reshape | solution.py:113
  194.9 35.8 %copy.99 = f32[2,8,512,1024]{3,2,1,0:T(8,128)} copy(f32[2,8,512,1024]{3,1,2,0:T(8,128)S(1)} %bitcast.264) | data formatting | bytes 67108864
  272.9 77.9 %concatenate.9 = f32[12,512,1025]{1,2,0:T(8,128)} concatenate(f32[12,512,1]{1,2,0:T(1,128)S(1)} %copy-done.76, f32[12,512,256]{1,2,0:T(8,128)} %broadcast_in_dim.46, f32[12,512,512]{1,2,0:T(8,128)} %copy-done.5, f32[12,512,256]{1,2,0:T(8,128)} %broadcast_in_dim.48), dimensions={2} | concatenate | bytes 50380800 | tf_op jit(solution)/shard_map/concatenate | solution.py:111
  350.8 25.9 %copy.55 = f32[12,512,1025]{2,1,0:T(8,128)} copy(f32[12,512,1025]{1,2,0:T(8,128)} %concatenate.9) | data formatting | bytes 50380800 | tf_op jit(solution)/shard_map/concatenate | solution.py:111
  376.7 40.8 %reshape.222 = f32[12,524800]{1,0:T(8,128)} reshape(f32[12,512,1025]{2,1,0:T(8,128)} %copy.55) | data formatting | bytes 50380800 | tf_op jit(solution)/shard_map/reshape | solution.py:113
  428.1 36.0 %copy.100 = f32[2,8,512,1024]{3,2,1,0:T(8,128)} copy(f32[2,8,512,1024]{3,1,2,0:T(8,128)S(1)} %bitcast.265) | data formatting | bytes 67108864
  464.2 18.1 %slice.204 = f32[12,512,1024]{2,1,0:T(8,128)} slice(f32[16,512,1024]{2,1,0:T(8,128)} %bitcast.266), slice={[0:12], [0:512], [0:1024]} | slice | bytes 50331648 | tf_op jit(solution)/shard_map/reshape | solution.py:114
  516.3 22.5 %all-gather.3.cloned.1.call-done = bf16[2048,768]{1,0:T(8,128)(2,1)} async-done(((bf16[512,768]{1,0:T(8,128)(2,1)}), bf16[2048,768]{1,0:T(8,128)(2,1)}) %all-gather.3.cloned.1.call-update) | async-done | bytes 3145744 | tf_op jit(solution)/shard_map/all_gather | solution.py:284
  543.8 15.9 %fusion.13 = (bf16[2048,768]{1,0:T(8,128)(2,1)S(1)}, f32[2048,768]{1,0:T(8,128)}) fusion(f32[2048,768]{1,0:T(8,128)S(1)} %fusion.113, bf16[2048,12]{0,1:T(8,128)(2,1)S(1)} %all_gather.13, bf16[12,768]{1,0:T(8,128)(2,1)S(1)} %copy-done.115), kind=kOutput, calls=%fused_computation.23 | convolution fusion | flops 141557760 | bytes 15796224 | tf_op jit(solution)/shard_map/dot_general | solution.py:20
  582.6 40.7 %reduce-scatter.5.cloned.1.call-done = bf16[512,768]{1,0:T(8,128)(2,1)} async-done(((bf16[2048,768]{1,0:T(8,128)(2,1)}), bf16[512,768]{1,0:T(8,128)(2,1)}) %reduce-scatter.5.cloned.1.call-update) | async-done | bytes 786448 | tf_op jit(solution)/shard_map/reduce_scatter | solution.py:290
  637.1 20.5 %all-gather.5.cloned.1.call-done = bf16[2048,768]{1,0:T(8,128)(2,1)} async-done(((bf16[512,768]{1,0:T(8,128)(2,1)}), bf16[2048,768]{1,0:T(8,128)(2,1)}) %all-gather.5.cloned.1.call-update) | async-done | bytes 3145744 | tf_op jit(solution)/shard_map/all_gather | solution.py:315
  684.0 38.0 %all-reduce.10 = (bf16[12,768]{1,0:T(8,128)(2,1)S(1)}, bf16[768,12]{0,1:T(8,128)(2,1)S(1)}) all-reduce(bf16[12,768]{1,0:T(8,128)(2,1)S(1)} %convolution_convert_fusion.5, bf16[768,12]{0,1:T(8,128)(2,1)S(1)} %convolution_convert_fusion.4), channel_id=1, replica_groups=mesh['dp'=8,'tensor'=4] {'dp'}, use_global_device_ids=true, to_apply=%region_29.30 | all-reduce | flops 18432 | bytes 73728 | tf_op jit(solution)/shard_map/psum | solution.py:429
  726.3 25.4 %reduce-scatter.9.cloned.1.call-done = f32[512,768]{1,0:T(8,128)} async-done(((f32[2048,768]{1,0:T(8,128)}), f32[512,768]{1,0:T(8,128)}) %reduce-scatter.9.cloned.1.call-update) | async-done | bytes 1572880 | tf_op jit(solution)/shard_map/reduce_scatter | solution.py:325
  809.9 29.2 %copy.101 = bf16[2,8,512,1024]{3,1,2,0:T(8,128)(2,1)S(1)} copy(bf16[2,8,512,1024]{3,2,1,0:T(8,128)(2,1)S(1)} %bitcast.268) | data formatting | bytes 33554432
  845.8 67.3 %reshape.228 = bf16[12,512,1025]{2,1,0:T(8,128)(2,1)} reshape(bf16[12,524800]{1,0:T(8,128)(2,1)} %pad.29) | data formatting | bytes 25190400 | tf_op jit(solution)/shard_map/reshape | solution.py:124
  926.6 16.6 %copy.96 = bf16[12,512,1024]{1,2,0:T(8,128)(2,1)} copy(bf16[12,512,1024]{2,1,0:T(8,128)(2,1)} %slice.195) | data formatting | bytes 25165824
  943.3 14.5 convert_element_type.222
  983.0 29.2 %copy.102 = bf16[2,8,512,1024]{3,1,2,0:T(8,128)(2,1)S(1)} copy(bf16[2,8,512,1024]{3,2,1,0:T(8,128)(2,1)S(1)} %bitcast.270) | data formatting | bytes 33554432
  1018.9 70.2 %reshape.231 = bf16[12,512,1025]{2,1,0:T(8,128)(2,1)} reshape(bf16[12,524800]{1,0:T(8,128)(2,1)} %pad.33) | data formatting | bytes 25190400 | tf_op jit(solution)/shard_map/reshape | solution.py:124
  1102.6 16.6 %copy.97 = bf16[12,512,1024]{1,2,0:T(8,128)(2,1)} copy(bf16[12,512,1024]{2,1,0:T(8,128)(2,1)} %slice.199) | data formatting | bytes 25165824
  1212.2 122.3 %all-reduce.16.cloned.1.call-done = (f32[4,768,12]{1,2,0:T(8,128)}, f32[4,12,768]{2,1,0:T(8,128)}) async-done(((f32[4,768,12]{1,2,0:T(8,128)}, f32[4,12,768]{2,1,0:T(8,128)}), (f32[4,768,12]{1,2,0:T(8,128)}, f32[4,12,768]{2,1,0:T(8,128)})) %all-reduce.16.cloned.1.call-update) | async-done | bytes 294928 | tf_op jit(solution)/shard_map/psum | solution.py:424
  1337.9 126.1 %all-reduce.14.cloned.1.call-done = (f32[4,12]{1,0:T(4,128)}, f32[768,12]{0,1:T(8,128)}, f32[2,12]{1,0:T(2,128)}, f32[12,768]{1,0:T(8,128)}) async-done(((f32[4,12]{1,0:T(4,128)}, f32[768,12]{0,1:T(8,128)}, f32[2,12]{1,0:T(2,128)}, f32[12,768]{1,0:T(8,128)}), (f32[4,12]{1,0:T(4,128)}, f32[768,12]{0,1:T(8,128)}, f32[2,12]{1,0:T(2,128)}, f32[12,768]{1,0:T(8,128)})) %all-reduce.14.cloned.1.call-update) | async-done | bytes 74032 | tf_op jit(solution)/shard_map/psum | solution.py:424
  (478 shorter events, 425.7 us)
Async XLA Ops:
  7.2 555.9 %copy-start = (bf16[768,768]{1,0:T(8,128)(2,1)S(1)}, bf16[768,768]{1,0:T(8,128)(2,1)}, u32[]{:S(2)}) copy-start(bf16[768,768]{1,0:T(8,128)(2,1)} %param.33) | copy-start | bytes 3538948
  7.2 531.6 %all-gather.3.cloned.1.call-start = ((), (), s32[]{:S(2)}) async-start(), calls=%async_computation.4 | async-start | bytes 3932160 | tf_op jit(solution)/shard_map/all_gather | solution.py:284
  23.8 230.3 %copy-start.109 = (f32[12]{0:T(128)}, f32[12]{0:T(128)S(1)}, u32[]{:S(2)}) copy-start(f32[12]{0:T(128)S(1)} %get-tuple-element.67) | copy-start | bytes 148
  23.8 232.5 %copy-start.111 = (f32[12]{0:T(128)}, f32[12]{0:T(128)S(1)}, u32[]{:S(2)}) copy-start(f32[12]{0:T(128)S(1)} %get-tuple-element.68) | copy-start | bytes 148
  39.5 77.9 %copy-start.75 = (f32[12,512,1]{1,2,0:T(1,128)}, f32[12,512,1]{1,2,0:T(1,128)S(1)}, u32[]{:S(2)}) copy-start(f32[12,512,1]{1,2,0:T(1,128)S(1)} %broadcast.143) | copy-start | bytes 73732
  505.2 118.1 %copy-start.97 = (f32[512]{0:T(512)}, f32[512]{0:T(512)S(1)}, u32[]{:S(2)}) copy-start(f32[512]{0:T(512)S(1)} %broadcast_multiply_fusion.5) | copy-start | bytes 6148
  505.5 117.8 %copy-start.103 = (f32[512]{0:T(512)}, f32[512]{0:T(512)S(1)}, u32[]{:S(2)}) copy-start(f32[512]{0:T(512)S(1)} %add_rsqrt_fusion.1) | copy-start | bytes 6148
  506.2 117.1 %copy-start.99 = (f32[768]{0:T(1024)}, f32[768]{0:T(1024)S(1)}, u32[]{:S(2)}) copy-start(f32[768]{0:T(1024)S(1)} %get-tuple-element.101) | copy-start | bytes 9220
  507.4 75.1 %reduce-scatter.7.cloned.1.call-start = ((), (), s32[]{:S(2)}) async-start(), calls=%async_computation.6 | async-start | bytes 81920 | tf_op jit(solution)/shard_map/reduce_scatter | solution.py:296
  563.0 60.3 %reduce-scatter.5.cloned.1.call-start = ((), (), s32[]{:S(2)}) async-start(), calls=%async_computation.5 | async-start | bytes 3932160 | tf_op jit(solution)/shard_map/reduce_scatter | solution.py:290
  569.3 88.3 %all-gather.5.cloned.1.call-start = ((), (), s32[]{:S(2)}) async-start(), calls=%async_computation.7 | async-start | bytes 3932160 | tf_op jit(solution)/shard_map/all_gather | solution.py:315
  628.9 94.3 %reduce-scatter.11.cloned.1.call-start = ((), (), s32[]{:S(2)}) async-start(), calls=%async_computation.9 | async-start | bytes 163840 | tf_op jit(solution)/shard_map/reduce_scatter | solution.py:328
  671.1 80.6 %reduce-scatter.9.cloned.1.call-start = ((), (), s32[]{:S(2)}) async-start(), calls=%async_computation.8 | async-start | bytes 7864320 | tf_op jit(solution)/shard_map/reduce_scatter | solution.py:325
  678.6 655.9 %all-reduce.16.cloned.1.call-start = ((), (), s32[]{:S(2)}) async-start(), calls=%async_computation.11 | async-start | bytes 786432 | tf_op jit(solution)/shard_map/psum | solution.py:424
  680.9 70.9 %copy-start.96 = (bf16[768,12]{0,1:T(8,128)(2,1)S(1)}, bf16[768,12]{0,1:T(8,128)(2,1)}, u32[]{:S(2)}) copy-start(bf16[768,12]{0,1:T(8,128)(2,1)} %param.31) | copy-start | bytes 55300
  680.9 70.8 %copy-start.98 = (f32[512]{0:T(512)S(1)}, f32[512]{0:T(512)}, u32[]{:S(2)}) copy-start(f32[512]{0:T(512)} %copy-done.97) | copy-start | bytes 6148
  680.9 70.8 %copy-start.100 = (f32[768]{0:T(1024)S(1)}, f32[768]{0:T(1024)}, u32[]{:S(2)}) copy-start(f32[768]{0:T(1024)} %copy-done.99) | copy-start | bytes 9220
  680.9 70.8 %copy-start.102 = (f32[768]{0:T(1024)S(1)}, f32[768]{0:T(1024)}, u32[]{:S(2)}) copy-start(f32[768]{0:T(1024)} %get-tuple-element.102) | copy-start | bytes 9220
  680.9 70.8 %copy-start.104 = (f32[512]{0:T(512)S(1)}, f32[512]{0:T(512)}, u32[]{:S(2)}) copy-start(f32[512]{0:T(512)} %copy-done.103) | copy-start | bytes 6148
  680.9 70.8 %copy-start.106 = (f32[512]{0:T(512)S(1)}, f32[512]{0:T(512)}, u32[]{:S(2)}) copy-start(f32[512]{0:T(512)} %copy-done.105) | copy-start | bytes 6148
  680.9 70.8 %copy-start.108 = (f32[512]{0:T(512)S(1)}, f32[512]{0:T(512)}, u32[]{:S(2)}) copy-start(f32[512]{0:T(512)} %copy-done.107) | copy-start | bytes 6148
  680.9 70.8 %copy-start.118 = (f32[512]{0:T(512)S(1)}, f32[512]{0:T(512)}, u32[]{:S(2)}) copy-start(f32[512]{0:T(512)} %copy-done.117) | copy-start | bytes 6148
  1206.2 257.7 %all-reduce.14.cloned.1.call-start = ((), (), s32[]{:S(2)}) async-start(), calls=%async_computation.10 | async-start | bytes 202752 | tf_op jit(solution)/shard_map/psum | solution.py:424
  1207.0 262.3 %copy-start.1 = (bf16[768,768]{1,0:T(8,128)(2,1)S(1)}, bf16[768,768]{1,0:T(8,128)(2,1)}, u32[]{:S(2)}) copy-start(bf16[768,768]{1,0:T(8,128)(2,1)} %param.33) | copy-start | bytes 3538948
  (138 other events, 1299.1 us)
Sparse Core Ops, SparseCore 0:
  507.5 31.2 all-gather.2
  563.1 19.4 reduce-scatter.6
  585.3 37.9 reduce-scatter.4
  629.0 28.5 all-gather.4
  671.2 19.5 reduce-scatter.10
  693.3 58.3 reduce-scatter.8
  1206.4 128.0 all-reduce.15
  1342.8 121.1 all-reduce.13
where the time goes:
time: 1490 us; the launch traced here: 1480 us
  local copies, waits for them, and re-layouts  788 us (53%)
  waiting for transfers between devices  371 us (25%)
  matrix products  185 us (12%)
  other arithmetic  65.5 us (4%)
  blocking collectives  50.2 us (3%)
  between operations  16 us (1%)
    psum x2, waiting for transfers between devices, body(): lax.psum((local_left, local_scale, local_right, local_expand_left, local_...  248 us
    unnamed x322, local copies, waits for them, and re-layouts  215 us
    concatenate x4, local copies, waits for them, and re-layouts, relative_pick(): spread_rows = jnp.concatenate(pieces, axis=2)  208 us
    reshape x2, local copies, waits for them, and re-layouts, relative_fold(): flat_rows.reshape(groups, length, width)[:, :, 1:1 + 2 * length]  138 us
    reshape x2, local copies, waits for them, and re-layouts, relative_pick(): spread_rows.reshape(groups, length * width)[:, :length * (width - 1)]  81.9 us
    dot_general x24, matrix products, product(): return jnp.dot(left, right, preferred_element_type=jnp.float32)  55.7 us
    dot_general x20, matrix products, product_trail(): lax.dot_general(left, right, (((1,), (1,)), ((), ())), preferred_element_...  48.6 us
    reduce_scatter x1, waiting for transfers between devices, body(): lax.psum_scatter(product(active, shrink_weight).astype(jnp.bfloat16), 'te...  40.7 us
  transfers between devices with their start and end apart: 8, of which 7 were waited for; matrix products, arithmetic and copies ran while one was open for 2% of the time, Pallas kernels for 0%

commit v1 on v0

v1 whole, which is shorter than its diff:
```python
import math

import jax
import jax.numpy as jnp
from jax import lax
from jax.experimental import pallas as pl
from jax.experimental.pallas import tpu as pltpu
from jax.sharding import PartitionSpec as P

PAIRS = 6
LANES = 128
ROWS = 512
WIDTH = 768
RANK = 12
BLOCKS = ROWS // LANES

norm_eps = 1e-07
masked_fill = -1e30
score_scale = 1.0 / math.sqrt(192.0)
inverse_root_two = 1.0 / math.sqrt(2.0)
inverse_root_tau = 1.0 / math.sqrt(2.0 * math.pi)

f32 = jnp.float32
bf16 = jnp.bfloat16


def dot_nn(left, right):
    return jnp.dot(left, right, preferred_element_type=f32)


def dot_nt(left, right):
    return lax.dot_general(left, right, (((1,), (1,)), ((), ())), preferred_element_type=f32)


def dot_tn(left, right):
    return lax.dot_general(left, right, (((0,), (0,)), ((), ())), preferred_element_type=f32)


def column_of(row):
    n = row.shape[1]
    eye = lax.broadcasted_iota(jnp.int32, (n, n), 0) == lax.broadcasted_iota(jnp.int32, (n, n), 1)
    return jnp.sum(jnp.where(eye, row, 0.0), axis=1, keepdims=True)


def block_iotas():
    shape = (LANES, LANES)
    return lax.broadcasted_iota(jnp.int32, shape, 0), lax.broadcasted_iota(jnp.int32, shape, 1)


def head_mask(which):
    lane = lax.broadcasted_iota(jnp.int32, (1, LANES), 1)
    return ((lane >= 64) if which else (lane < 64)).astype(bf16)


def pick_tiles(scores, block, below):
    first = scores[:, :1]
    last = scores[:, ROWS - 1 :]
    rolled = pltpu.roll(scores, 1, 1, stride=1, stride_axis=0)
    tiles = []
    for other in range(BLOCKS):
        v = other - block + 2
        if v < 0:
            tile = jnp.broadcast_to(first, (LANES, LANES))
        elif v == 0:
            tile = jnp.where(below, first, rolled[:, :LANES])
        elif v < 4:
            tile = rolled[:, v * LANES : (v + 1) * LANES]
        elif v == 4:
            tile = jnp.where(below, rolled[:, :LANES], last)
        else:
            tile = jnp.broadcast_to(last, (LANES, LANES))
        tiles.append(tile)
    return tiles


def fold_rows(grads, block, below_rev, lane_first, lane_last):
    zero = jnp.zeros((LANES, LANES), f32)
    tile = [grads[:, b * LANES : (b + 1) * LANES] for b in range(BLOCKS)]
    placed = [zero, zero, zero, zero]
    low = None
    high = None
    for other in range(BLOCKS):
        v = other - block + 2
        if v < 0:
            low = tile[other] if low is None else low + tile[other]
        elif v == 0:
            placed[0] = jnp.where(below_rev, 0.0, tile[other])
            part = jnp.where(below_rev, tile[other], 0.0)
            low = part if low is None else low + part
        elif v < 4:
            placed[v] = tile[other]
        elif v == 4:
            placed[0] = jnp.where(below_rev, tile[other], 0.0)
            part = jnp.where(below_rev, 0.0, tile[other])
            high = part if high is None else high + part
        else:
            high = tile[other] if high is None else high + tile[other]
    rolled = pltpu.roll(
        jnp.concatenate(placed, axis=1), ROWS - LANES, 1, stride=1, stride_axis=0
    )
    out = [rolled[:, b * LANES : (b + 1) * LANES] for b in range(BLOCKS)]
    if low is not None:
        out[0] = out[0] + jnp.where(lane_first, jnp.sum(low, axis=1, keepdims=True), 0.0)
    if high is not None:
        out[3] = out[3] + jnp.where(lane_last, jnp.sum(high, axis=1, keepdims=True), 0.0)
    return jnp.concatenate(out, axis=1)


def attend_kernel(
    segment,
    live,
    tokens,
    table,
    mix_weight,
    left_t,
    right,
    scale,
    shares_out,
    q_s,
    k_s,
    v_s,
    tq_s,
    tk_s,
    tr_s,
    context_out,
    shares_s,
    bias_s,
    across_s,
    sems,
):
    row, lane = block_iotas()
    below = lane <= row
    flip = (row + lane == LANES - 1).astype(bf16)
    seg_row = segment[...]
    key_row = jnp.where(live[...] == 1, seg_row, -1)
    for a in range(BLOCKS):
        seg_col = jnp.broadcast_to(
            seg_row[:, a * LANES : (a + 1) * LANES].astype(f32), (LANES, LANES)
        ).T.astype(jnp.int32)
        for b in range(BLOCKS):
            same = seg_col == key_row[:, b * LANES : (b + 1) * LANES]
            if a == b:
                same = same | (row == lane)
            bias_s[a * LANES : (a + 1) * LANES, b * LANES : (b + 1) * LANES] = jnp.where(
                same, 0.0, masked_fill
            )
    for a in range(BLOCKS):
        tr_s[a * LANES : (a + 1) * LANES, :] = dot_nn(
            flip, table[(3 - a) * LANES : (4 - a) * LANES, :]
        ).astype(bf16)

    def project(source, which, target):
        rank_t = dot_nt(left_t[:, which, :], source)
        low_t = (rank_t * column_of(scale[which : which + 1, :])).astype(bf16)
        full = dot_nn(source, mix_weight[which]) + dot_tn(low_t, right[:, which, :])
        for p in range(PAIRS):
            target[p] = full[:, p * LANES : (p + 1) * LANES].astype(bf16)

    project(tokens[...], 0, q_s)
    project(tokens[...], 1, k_s)
    project(tokens[...], 2, v_s)
    project(tr_s[...], 0, tq_s)
    project(tr_s[...], 1, tk_s)

    def pair(p, carry):
        kp = k_s[p]
        tq = tq_s[p]
        tk = tk_s[p]
        context = [None] * BLOCKS
        for which in range(2):
            mask = head_mask(which)
            for b in range(BLOCKS):
                scores = dot_nt(k_s[p, b * LANES : (b + 1) * LANES, :] * mask, tq)
                tiles = pick_tiles(scores, b, below)
                for a in range(BLOCKS):
                    across_s[a * LANES : (a + 1) * LANES, b * LANES : (b + 1) * LANES] = tiles[a].T
            vm = v_s[p] * mask
            for a in range(BLOCKS):
                rows = slice(a * LANES, (a + 1) * LANES)
                qm = q_s[p, rows, :] * mask
                tiles = pick_tiles(dot_nt(qm, tk), a, below)
                total = (
                    dot_nt(qm, kp)
                    + jnp.concatenate(tiles, axis=1)
                    + across_s[rows, :]
                    + bias_s[rows, :]
                )
                peak = jnp.max(total, axis=1, keepdims=True)
                weights = jnp.exp((total - peak) * score_scale)
                inverse = 1.0 / jnp.sum(weights, axis=1, keepdims=True)
                low = (weights * inverse).astype(bf16)
                shares_s[p, which, rows, :] = low
                part = dot_nn(low, vm)
                context[a] = part if which == 0 else context[a] + part
        for a in range(BLOCKS):
            context_out[p, a * LANES : (a + 1) * LANES, :] = context[a].astype(bf16)
        pltpu.make_async_copy(shares_s.at[p], shares_out.at[p], sems.at[p]).start()
        return carry

    lax.fori_loop(0, PAIRS, pair, 0)

    def finish(p, carry):
        pltpu.make_async_copy(shares_s.at[p], shares_out.at[p], sems.at[p]).wait()
        return carry

    lax.fori_loop(0, PAIRS, finish, 0)


def vmem():
    return pl.BlockSpec(memory_space=pltpu.VMEM)


def attend(segment, live, tokens, table, mix_weight, left_t, right, scale):
    piece = jax.ShapeDtypeStruct((PAIRS, ROWS, LANES), bf16)
    return pl.pallas_call(
        attend_kernel,
        out_shape=(
            jax.ShapeDtypeStruct((PAIRS, 2, ROWS, ROWS), bf16),
            piece,
            piece,
            piece,
            piece,
            piece,
            jax.ShapeDtypeStruct((ROWS, WIDTH), bf16),
            piece,
        ),
        in_specs=[vmem()] * 8,
        out_specs=(pl.BlockSpec(memory_space=pl.ANY),) + (vmem(),) * 7,
        scratch_shapes=[
            pltpu.VMEM((PAIRS, 2, ROWS, ROWS), bf16),
            pltpu.VMEM((ROWS, ROWS), f32),
            pltpu.VMEM((ROWS, ROWS), f32),
            pltpu.SemaphoreType.DMA((PAIRS,)),
        ],
        compiler_params=pltpu.CompilerParams(vmem_limit_bytes=56 * 2**20),
        name="attend",
    )(segment, live, tokens, table, mix_weight, left_t, right, scale)


def norm_parts(values):
    center = values - jnp.mean(values, axis=-1, keepdims=True)
    root = lax.rsqrt(jnp.mean(center * center, axis=-1, keepdims=True) + norm_eps)
    return center * root, root


def norm_back(scaled, unit, root):
    return root * (
        scaled
        - jnp.mean(scaled, axis=-1, keepdims=True)
        - unit * jnp.mean(scaled * unit, axis=-1, keepdims=True)
    )


def feed_kernel(
    context,
    tokens,
    cotangent,
    out_weight,
    left_t,
    right,
    scale,
    gain,
    shift,
    expand,
    expand_left_t,
    expand_right,
    shrink,
    shrink_left_t,
    shrink_right,
    feed_scale,
    layer_out,
    grad_first_out,
    grad_context_out,
    out_left_grad,
    out_right_grad,
    expand_left_grad,
    shrink_right_grad,
    expand_right_grad,
    shrink_left_grad,
    scales_out,
    x_s,
    normed_s,
    hidden_s,
    act_s,
    slope_s,
    branch_s,
    context_s,
):
    chunks = expand.shape[0]
    wide = lax.broadcasted_iota(jnp.int32, (RANK, LANES), 1)
    lam_out = column_of(scale[3:4, :])
    lam_one = column_of(feed_scale[0:1, :])
    lam_two = column_of(feed_scale[1:2, :])
    step = LANES
    steps = ROWS // step

    for p in range(PAIRS):
        context_s[:, p * LANES : (p + 1) * LANES] = context[p]
    out_rank = dot_nt(left_t[:, 3, :], context_s[...])
    out_low = (out_rank * lam_out).astype(bf16)
    x_s[...] = dot_nn(context_s[...], out_weight[...]) + dot_tn(out_low, right[:, 3, :])

    def first_norm(i, carry):
        rows = pl.ds(i * step, step)
        values = tokens[rows, :].astype(f32) + x_s[rows, :]
        x_s[rows, :] = values
        unit, root = norm_parts(values)
        normed = unit * gain[0:1, :] + shift[0:1, :]
        normed_s[rows, :] = normed
        hidden_s[rows, :] = normed.astype(bf16)
        return carry

    lax.fori_loop(0, steps, first_norm, 0)

    one_rank = dot_nt(expand_left_t[...], hidden_s[...])
    one_low = (one_rank * lam_one).astype(bf16)
    branch_s[...] = jnp.zeros_like(branch_s)

    def forward(c, two_rank):
        pre = dot_nn(hidden_s[...], expand[c]) + dot_tn(one_low, expand_right[c])
        cdf = 0.5 + 0.5 * lax.erf(pre * inverse_root_two)
        act = (pre * cdf).astype(bf16)
        act_s[c] = act
        slope_s[c] = cdf + pre * jnp.exp(-0.5 * pre * pre) * inverse_root_tau
        branch_s[...] += dot_nn(act, shrink[c])
        return two_rank + dot_nt(shrink_left_t[c], act)

    two_rank = lax.fori_loop(0, chunks, forward, jnp.zeros((RANK, ROWS), f32))
    two_low = (two_rank * lam_two).astype(bf16)
    branch_s[...] += dot_tn(two_low, shrink_right[...])

    def second_norm(i, carry):
        rows = pl.ds(i * step, step)
        unit, root = norm_parts(normed_s[rows, :] + branch_s[rows, :])
        layer_out[rows, :] = (unit * gain[1:2, :] + shift[1:2, :]).astype(bf16)
        grad = norm_back(cotangent[rows, :].astype(f32) * gain[1:2, :], unit, root)
        branch_s[rows, :] = grad
        return carry

    lax.fori_loop(0, steps, second_norm, 0)
    grad_branch = branch_s[...].astype(bf16)
    two_back = dot_nt(shrink_right[...], grad_branch)
    two_small = (two_back * lam_two).astype(bf16)
    shrink_right_grad[...] = dot_nn(two_low, grad_branch)
    two_scale = jnp.sum(two_rank * two_back, axis=1, keepdims=True)

    def backward(c, one_back):
        grad_act = dot_nt(grad_branch, shrink[c]) + dot_tn(two_small, shrink_left_t[c])
        grad_pre = (grad_act * slope_s[c]).astype(bf16)
        shrink_left_grad[c] = dot_nn(two_small, act_s[c])
        expand_right_grad[c] = dot_nn(one_low, grad_pre)
        branch_s[...] += dot_nt(grad_pre, expand[c])
        return one_back + dot_nt(expand_right[c], grad_pre)

    one_back = lax.fori_loop(0, chunks, backward, jnp.zeros((RANK, ROWS), f32))
    one_small = (one_back * lam_one).astype(bf16)
    branch_s[...] += dot_tn(one_small, expand_left_t[...])
    expand_left_grad[...] = dot_nn(one_small, hidden_s[...])
    one_scale = jnp.sum(one_rank * one_back, axis=1, keepdims=True)

    def first_back(i, carry):
        rows = pl.ds(i * step, step)
        unit, root = norm_parts(x_s[rows, :])
        grad_first_out[rows, :] = norm_back(branch_s[rows, :] * gain[0:1, :], unit, root)
        return carry

    lax.fori_loop(0, steps, first_back, 0)
    grad_attended = grad_first_out[...].astype(bf16)
    out_back = dot_nt(right[:, 3, :], grad_attended)
    out_small = (out_back * lam_out).astype(bf16)
    grad_context_out[...] = (
        dot_nt(grad_attended, out_weight[...]) + dot_tn(out_small, left_t[:, 3, :])
    ).astype(bf16)
    out_left_grad[...] = dot_nn(out_small, context_s[...])
    out_right_grad[...] = dot_nn(out_low, grad_attended)
    out_scale = jnp.sum(out_rank * out_back, axis=1, keepdims=True)
    scales_out[...] = jnp.where(
        wide == 3,
        out_scale,
        jnp.where(wide == 4, one_scale, jnp.where(wide == 5, two_scale, 0.0)),
    )


def feed(*args):
    chunks, _, hidden = args[9].shape
    small = jax.ShapeDtypeStruct((RANK, WIDTH), f32)
    parts = jax.ShapeDtypeStruct((chunks, RANK, hidden), f32)
    return pl.pallas_call(
        feed_kernel,
        out_shape=(
            jax.ShapeDtypeStruct((ROWS, WIDTH), bf16),
            jax.ShapeDtypeStruct((ROWS, WIDTH), f32),
            jax.ShapeDtypeStruct((ROWS, WIDTH), bf16),
            small,
            small,
            small,
            small,
            parts,
            parts,
            jax.ShapeDtypeStruct((RANK, LANES), f32),
        ),
        in_specs=[vmem()] * 16,
        out_specs=(vmem(),) * 10,
        scratch_shapes=[
            pltpu.VMEM((ROWS, WIDTH), f32),
            pltpu.VMEM((ROWS, WIDTH), f32),
            pltpu.VMEM((ROWS, WIDTH), bf16),
            pltpu.VMEM((chunks, ROWS, hidden), bf16),
            pltpu.VMEM((chunks, ROWS, hidden), f32),
            pltpu.VMEM((ROWS, WIDTH), f32),
            pltpu.VMEM((ROWS, WIDTH), bf16),
        ],
        compiler_params=pltpu.CompilerParams(vmem_limit_bytes=58 * 2**20),
        name="feed",
    )(*args)


def back_kernel(
    grad_context,
    grad_first,
    shares_in,
    q_s,
    k_s,
    v_s,
    tq_s,
    tk_s,
    tr_s,
    tokens,
    mix_weight,
    left_t,
    right,
    scale,
    grad_tokens,
    left_grad,
    right_grad,
    scales_out,
    shares_s,
    gl_s,
    qf_s,
    kf_s,
    fq_s,
    fk_s,
    gq_s,
    gk_s,
    gv_t,
    gtq_t,
    gtk_t,
    sems,
):
    row, lane = block_iotas()
    below_rev = lane + row <= LANES - 1
    lane_first = lane == 0
    lane_last = lane == LANES - 1
    flip = (row + lane == LANES - 1).astype(bf16)

    def begin(p, carry):
        pltpu.make_async_copy(shares_in.at[p], shares_s.at[p], sems.at[p]).start()
        return carry

    lax.fori_loop(0, PAIRS, begin, 0)

    def flipped(values):
        return jnp.concatenate(
            [
                dot_nn(flip, values[b * LANES : (b + 1) * LANES, :]).astype(bf16)
                for b in range(BLOCKS)
            ],
            axis=0,
        )

    def pair(p, carry):
        pltpu.make_async_copy(shares_in.at[p], shares_s.at[p], sems.at[p]).wait()
        gc = grad_context[p]
        gc_t = gc.T
        q_rev_t = flipped(q_s[p]).T
        k_rev_t = flipped(k_s[p]).T
        vp = v_s[p]
        gq = None
        gk = None
        for which in range(2):
            mask = head_mask(which)
            half = slice(which * 64, which * 64 + 64)
            for a in range(BLOCKS):
                rows = slice(a * LANES, (a + 1) * LANES)
                shares = shares_s[p, which, rows, :].astype(f32)
                grad = dot_nt(gc[rows, :] * mask, vp)
                prod = grad * shares
                inner = jnp.sum(prod, axis=1, keepdims=True)
                gl_s[rows, :] = (prod - shares * inner).astype(bf16)
            for a in range(BLOCKS):
                rows = slice(a * LANES, (a + 1) * LANES)
                along = dot_nn(flip, gl_s[rows, :])
                qf_s[rows, :] = along.astype(bf16)
                fq_s[rows, :] = (
                    fold_rows(along, a, below_rev, lane_first, lane_last) * score_scale
                ).astype(bf16)
                across = dot_nt(flip, gl_s[:, rows])
                kf_s[rows, :] = across.astype(bf16)
                fk_s[rows, :] = (
                    fold_rows(across, a, below_rev, lane_first, lane_last) * score_scale
                ).astype(bf16)
            fq = fq_s[...]
            fk = fk_s[...]
            part_q = dot_nn(qf_s[...], k_s[p] * mask) * score_scale + dot_nn(fq, tk_s[p] * mask)
            part_k = dot_nn(kf_s[...], q_s[p] * mask) * score_scale + dot_nn(fk, tq_s[p] * mask)
            gq = part_q if which == 0 else gq + part_q
            gk = part_k if which == 0 else gk + part_k
            out = pl.ds(pl.multiple_of(p * LANES + which * 64, 64), 64)
            gv_t[out, :] = dot_nn(gc_t[half, :], shares_s[p, which]).astype(bf16)
            gtk_t[out, :] = dot_nn(q_rev_t[half, :], fq).astype(bf16)
            gtq_t[out, :] = dot_nn(k_rev_t[half, :], fk).astype(bf16)
        gq_s[p] = flipped(gq.astype(bf16))
        gk_s[p] = flipped(gk.astype(bf16))
        return carry

    lax.fori_loop(0, PAIRS, pair, 0)

    wide = lax.broadcasted_iota(jnp.int32, (RANK, LANES), 1)
    total = grad_first[...]
    scales = jnp.zeros((RANK, LANES), f32)
    source = tokens[...]
    for which in range(3):
        if which == 2:
            grad = gv_t[...].T
        else:
            grad = jnp.concatenate([(gq_s, gk_s)[which][p] for p in range(PAIRS)], axis=1)
        left = left_t[:, which, :]
        lam = column_of(scale[which : which + 1, :])
        rank = dot_nt(left, source)
        low = (rank * lam).astype(bf16)
        back = dot_nt(right[:, which, :], grad)
        small = (back * lam).astype(bf16)
        total = total + dot_nt(grad, mix_weight[which]) + dot_tn(small, left)
        left_sum = dot_nn(small, source)
        right_sum = dot_nn(low, grad)
        scale_sum = jnp.sum(rank * back, axis=1, keepdims=True)
        if which < 2:
            table_grad = (gtq_t, gtk_t)[which][...]
            rank = dot_nt(left, tr_s[...])
            low = (rank * lam).astype(bf16)
            back = dot_nn(right[:, which, :], table_grad)
            small = (back * lam).astype(bf16)
            left_sum = left_sum + dot_nn(small, tr_s[...])
            right_sum = right_sum + dot_nt(low, table_grad)
            scale_sum = scale_sum + jnp.sum(rank * back, axis=1, keepdims=True)
        left_grad[which] = left_sum
        right_grad[which] = right_sum
        scales = jnp.where(wide == which, scale_sum, scales)
    grad_tokens[...] = total
    scales_out[...] = scales


def back(*args):
    sums = jax.ShapeDtypeStruct((3, RANK, WIDTH), f32)
    return pl.pallas_call(
        back_kernel,
        out_shape=(
            jax.ShapeDtypeStruct((ROWS, WIDTH), f32),
            sums,
            sums,
            jax.ShapeDtypeStruct((RANK, LANES), f32),
        ),
        in_specs=[vmem(), vmem(), pl.BlockSpec(memory_space=pl.ANY)] + [vmem()] * 11,
        out_specs=(vmem(),) * 4,
        scratch_shapes=[
            pltpu.VMEM((PAIRS, 2, ROWS, ROWS), bf16),
            pltpu.VMEM((ROWS, ROWS), bf16),
            pltpu.VMEM((ROWS, ROWS), bf16),
            pltpu.VMEM((ROWS, ROWS), bf16),
            pltpu.VMEM((ROWS, ROWS), bf16),
            pltpu.VMEM((ROWS, ROWS), bf16),
            pltpu.VMEM((PAIRS, ROWS, LANES), bf16),
            pltpu.VMEM((PAIRS, ROWS, LANES), bf16),
            pltpu.VMEM((WIDTH, ROWS), bf16),
            pltpu.VMEM((WIDTH, ROWS), bf16),
            pltpu.VMEM((WIDTH, ROWS), bf16),
            pltpu.SemaphoreType.DMA((PAIRS,)),
        ],
        compiler_params=pltpu.CompilerParams(vmem_limit_bytes=58 * 2**20),
        name="back",
    )(*args)


def body(
    tokens,
    segment,
    live,
    mix_weight,
    out_weight,
    position_table,
    norm_gain,
    norm_bias,
    mix_left,
    mix_scale,
    mix_right,
    expand_weight,
    expand_left,
    expand_right,
    shrink_weight,
    shrink_left,
    feed_scale,
    shrink_right,
    cotangent,
):
    left_t = jnp.transpose(mix_left, (2, 0, 1))
    right = jnp.transpose(mix_right, (1, 0, 2))
    expand_all = lax.all_gather(expand_weight, "tensor")
    shrink_all = lax.all_gather(shrink_weight, "tensor")
    small_all = lax.all_gather(jnp.stack([expand_right, shrink_left.T]), "tensor")
    shares, q, k, v, tq, tk, tr, context = attend(
        segment.reshape(1, ROWS),
        live.reshape(1, ROWS),
        tokens,
        position_table,
        mix_weight,
        left_t,
        right,
        mix_scale,
    )
    (
        layer_out,
        grad_first,
        grad_context,
        out_left_g,
        out_right_g,
        expand_left_g,
        shrink_right_g,
        expand_right_g,
        shrink_left_g,
        feed_scales,
    ) = feed(
        context,
        tokens,
        cotangent,
        out_weight,
        left_t,
        right,
        mix_scale,
        norm_gain,
        norm_bias,
        expand_all,
        expand_left.T,
        small_all[:, 0],
        shrink_all,
        small_all[:, 1],
        shrink_right,
        feed_scale,
    )
    grad_pieces = jnp.transpose(grad_context.reshape(ROWS, PAIRS, LANES), (1, 0, 2))
    grad_tokens, left_g, right_g, mix_scales = back(
        grad_pieces,
        grad_first,
        shares,
        q,
        k,
        v,
        tq,
        tk,
        tr,
        tokens,
        mix_weight,
        left_t,
        right,
        mix_scale,
    )
    left_g = jnp.concatenate([left_g, out_left_g[None]])
    right_g = jnp.concatenate([right_g, out_right_g[None]])
    scales = feed_scales + mix_scales
    left_g, right_g, scales, expand_left_g, shrink_right_g, expand_right_g, shrink_left_g = lax.psum(
        (
            left_g,
            right_g,
            scales,
            expand_left_g,
            shrink_right_g,
            expand_right_g,
            shrink_left_g,
        ),
        ("dp", "tensor"),
    )
    me = lax.axis_index("tensor")
    return (
        layer_out,
        grad_tokens,
        jnp.transpose(left_g, (0, 2, 1)),
        scales[:, :4].T,
        right_g,
        expand_left_g.T,
        lax.dynamic_index_in_dim(expand_right_g, me, 0, keepdims=False),
        lax.dynamic_index_in_dim(shrink_left_g, me, 0, keepdims=False).T,
        scales[:, 4:6].T,
        shrink_right_g,
    )


def solution(mesh):
    rows = P(("dp", "tensor"), None)
    line = P(("dp", "tensor"))
    return jax.shard_map(
        body,
        mesh=mesh,
        in_specs=(
            rows,
            line,
            line,
            P(),
            P(),
            P(),
            P(),
            P(),
            P(),
            P(),
            P(),
            P(None, "tensor"),
            P(),
            P(None, "tensor"),
            P("tensor", None),
            P("tensor", None),
            P(),
            P(),
            rows,
        ),
        out_specs=(
            rows,
            rows,
            P(),
            P(),
            P(),
            P(),
            P(None, "tensor"),
            P("tensor", None),
            P(),
            P(),
        ),
        check_vma=False,
    )
```

time: 1490 us -> 451 us (0.30)
  local copies, waits for them, and re-layouts: 788 us -> 15.1 us
  matrix products: 185 us -> 0 us
  Pallas kernels: 0 us -> 123 us
  waiting for transfers between devices: 371 us -> 288 us
  other arithmetic: 65.5 us -> 3.09 us
  blocking collectives: 50.2 us -> 6.87 us
    reshape x5 -> x1, local copies, waits for them, and re-layouts: 238 us -> 1.19 us  [body(): grad_context.reshape(ROWS, PAIRS, LANES)]
    concatenate x4 -> x0, local copies, waits for them, and re-layouts: 208 us -> none  [relative_pick(): spread_rows = jnp.concatenate(pieces, axis=2)]
    unnamed x322 -> x16, local copies, waits for them, and re-layouts: 215 us -> 7.54 us
    dot_general x72 -> x0, matrix products: 185 us -> none  [the longest x24 55.7 us: product(): return jnp.dot(left, right, preferred_element_type=jnp.float32)]
    pallas_call x0 -> x3, Pallas kernels: none -> 123 us  [the longest x1 51.4 us: back(): pl.pallas_call(back_kernel, out_shape=(jax.ShapeDtypeStruct((ROWS, WIDTH)...]
    reduce_scatter x4 -> x0, waiting for transfers between devices: 79.4 us -> none  [the longest x1 40.7 us: body(): lax.psum_scatter(product(active, shrink_weight).astype(jnp.bfloat16), 'te...]
    slice x12 -> x0, local copies, waits for them, and re-layouts: 62 us -> none  [the longest x2 26.9 us: relative_fold(): flat_rows.reshape(groups, length, width)[:, :, 1:1 + 2 * length]]
    convert_element_type x7 -> x0, other arithmetic: 43 us -> none  [the longest x2 29 us: relative_fold(): flat_rows.reshape(groups, length, width)[:, :, 1:1 + 2 * length]]
  transfers between devices with their start and end apart: 8 -> 4, of which waited for: 7 -> 3; matrix products, arithmetic and copies ran while one was open for 2% -> 1% of each run, Pallas kernels for 0% -> 9%
where the time goes in v1:
time: 451 us
  waiting for transfers between devices  288 us (64%)
  Pallas kernels  123 us (27%)
  local copies, waits for them, and re-layouts  15.1 us (3%)
  between operations  13.9 us (3%)
  blocking collectives  6.87 us (2%)
    psum x2, waiting for transfers between devices, body(): lax.psum((left_g, right_g, scales, expand_left_g, shrink_right_g, expand_...  254 us
    pallas_call x1, Pallas kernels, back(): pl.pallas_call(back_kernel, out_shape=(jax.ShapeDtypeStruct((ROWS, WIDTH)...  51.4 us
    pallas_call x1, Pallas kernels, attend(): pl.pallas_call(attend_kernel, out_shape=(jax.ShapeDtypeStruct((PAIRS, 2,...  39.6 us
    all_gather x1, waiting for transfers between devices, body(): expand_all = lax.all_gather(expand_weight, 'tensor')  32.9 us
    pallas_call x1, Pallas kernels, feed(): pl.pallas_call(feed_kernel, out_shape=(jax.ShapeDtypeStruct((ROWS, WIDTH)...  32.4 us
  transfers between devices with their start and end apart: 4, of which 3 were waited for; matrix products, arithmetic and copies ran while one was open for 1% of the time, Pallas kernels for 9%

profile of v1, /device:TPU:0, one launch (start us, length us, event | category | flops | bytes accessed | tf_op | source)
XLA Modules:
  0.0 450.6 jit_solution(494790305430921767)
XLA Ops:
  7.2 0.7 all-gather.8.cloned.1.call-update
  8.0 0.7 all-gather.6.cloned.1.call-update
  8.7 39.6 %attend.1 = (bf16[6,2,512,512]{3,2,1,0:T(8,128)(2,1)}, bf16[6,512,128]{2,1,0:T(8,128)(2,1)}, bf16[6,512,128]{2,1,0:T(8,128)(2,1)}, bf16[6,512,128]{2,1,0:T(8,128...) custom-call(s32[1,512]{1,0:T(1,128)} %bitcast.54, ...), custom_call_target="tpu_custom_call" | custom-call | tf_op jit(solution)/shard_map/attend/pallas_call | solution.py:215
  48.3 6.9 %all-gather.1 = bf16[8,12,768]{2,1,0:T(8,128)(2,1)S(1)} all-gather(bf16[2,12,768]{2,1,0:T(8,128)(2,1)S(1)} %pad_maximum_fusion.1), channel_id=3, replica_groups=mesh['dp'=8,'tensor'=4] {'tensor'}, dimensions={0}, use_global_device_ids=true | all-gather | bytes 184320 | tf_op jit(solution)/shard_map/all_gather | solution.py:609
  55.2 0.7 slice_bitcast_fusion
  55.9 32.9 %all-gather.6.cloned.1.call-done = bf16[3072,768]{1,0:T(8,128)(2,1)} async-done(((bf16[768,768]{1,0:T(8,128)(2,1)}), bf16[3072,768]{1,0:T(8,128)(2,1)}) %all-gather.6.cloned.1.call-update) | async-done | bytes 4718608 | tf_op jit(solution)/shard_map/all_gather | solution.py:607
  88.8 32.4 %feed.1 = (bf16[512,768]{1,0:T(8,128)(2,1)}, f32[512,768]{1,0:T(8,128)}, bf16[512,768]{1,0:T(8,128)(2,1)}, f32[12,768]{1,0:T(8,128)}, f32[12,768]{1,0:T(8,128)},...) custom-call(bf16[6,512,128]{2,1,0:T(8,128)(2,1)} %get-tuple-element., ...), custom_call_target="tpu_custom_call" | custom-call | tf_op jit(solution)/shard_map/feed/pallas_call | solution.py:388
  121.2 1.4 copy.45
  122.6 1.2 copy.46
  123.8 51.4 %back.1 = (f32[512,768]{1,0:T(8,128)}, f32[3,12,768]{2,1,0:T(8,128)}, f32[3,12,768]{2,1,0:T(8,128)}, f32[12,128]{1,0:T(8,128)}) custom-call(bf16[6,512,128]{2,1,0:T(8,128)(2,1)} %bitcast.39, f32[512,768]{1,0:T(8,128)} %get-tuple-element.35.grad_first, bf16[6,2,512,512]{3,2,1,0:T(8,128)(2,1)} %get-tuple-element.36.shares_in, ...), custom_call_target="tpu_custom_call" | custom-call | tf_op jit(solution)/shard_map/back/pallas_call | solution.py:555
  175.3 1.3 add.22
  176.6 1.8 maximum_bitcast_fusion
  178.4 120.2 %all-reduce.5.cloned.1.call-done = (f32[12,128]{1,0:T(8,128)}, f32[768,12]{0,1:T(8,128)}, f32[12,768]{1,0:T(8,128)}) async-done(((f32[12,128]{1,0:T(8,128)}, f32[768,12]{0,1:T(8,128)}, f32[12,768]{1,0:T(8,128)}), (f32[12,128]{1,0:T(8,128)}, f32[768,12]{0,1:T(8,128)}, f32[12,768]{1,0:T(8,128)})) %all-reduce.5.cloned.1.call-update) | async-done | bytes 79888 | tf_op jit(solution)/shard_map/psum | solution.py:669
  298.6 0.7 slice_bitcast_fusion.3
  299.3 0.7 copy.48
  300.0 0.8 slice_bitcast_fusion.2
  300.7 0.6 copy.50
  301.4 133.6 %all-reduce.7.cloned.1.call-done = (f32[4,768,12]{1,2,0:T(8,128)}, f32[4,12,768]{2,1,0:T(8,128)}, f32[4,12,768]{2,1,0:T(8,128)}, f32[4,12,768]{2,1,0:T(8,128)}) async-done(((f32[4,768,12]{1,2,0:T(8,128)}, f32[4,12,768]{2,1,0:T(8,128)}, f32[4,12,768]{2,1,0:T(8,128)}, f32[4,12,768]{2,1,0:T(8,128)}), (f32[4,768,12]{1,2,0:T(8,128)}, f32[4,12,768]{2,1,0:T(8,128)}, f32[4,12,768]{2,1,0:T(8,128)}, ...) | async-done | bytes 589840 | tf_op jit(solution)/shard_map/psum | solution.py:669
  435.0 1.7 copy.47
  436.7 1.7 copy.49
  438.4 1.4 dynamic-slice_bitcast_fusion
  439.8 1.4 dynamic-slice_bitcast_fusion.1
  441.2 1.4 copy.62
  442.7 1.4 copy.63
  (18 shorter events, 0.2 us)
Async XLA Ops:
  7.2 48.7 %all-gather.8.cloned.1.call-start = ((), (), s32[]{:S(2)}) async-start(), calls=%async_computation.1 | async-start | bytes 5898240 | tf_op jit(solution)/shard_map/all_gather | solution.py:608
  7.9 80.9 %all-gather.6.cloned.1.call-start = ((), (), s32[]{:S(2)}) async-start(), calls=%async_computation | async-start | bytes 5898240 | tf_op jit(solution)/shard_map/all_gather | solution.py:607
  8.7 289.9 %all-reduce.5.cloned.1.call-start = ((), (), s32[]{:S(2)}) async-start(), calls=%async_computation.2 | async-start | bytes 212992 | tf_op jit(solution)/shard_map/psum | solution.py:669
  8.7 39.6 %copy-start.2 = (bf16[768,12]{0,1:T(8,128)(2,1)S(1)}, bf16[768,12]{0,1:T(8,128)(2,1)}, u32[]{:S(2)}) copy-start(bf16[768,12]{0,1:T(8,128)(2,1)} %param.34) | copy-start | bytes 55300
  8.7 39.6 %copy-start.3 = (bf16[12,768]{1,0:T(8,128)(2,1)S(1)}, bf16[12,768]{1,0:T(8,128)(2,1)}, u32[]{:S(2)}) copy-start(bf16[12,768]{1,0:T(8,128)(2,1)} %param.32) | copy-start | bytes 55300
  123.8 51.5 %copy-start.4 = (f32[12,128]{1,0:T(8,128)S(1)}, f32[12,128]{1,0:T(8,128)}, u32[]{:S(2)}) copy-start(f32[12,128]{1,0:T(8,128)} %get-tuple-element.46) | copy-start | bytes 18436
  123.8 52.8 %copy-start = (f32[12,768]{1,0:T(8,128)S(1)}, f32[12,768]{1,0:T(8,128)}, u32[]{:S(2)}) copy-start(f32[12,768]{1,0:T(8,128)} %get-tuple-element.45) | copy-start | bytes 110596
  123.8 52.8 %copy-start.1 = (f32[12,768]{1,0:T(8,128)S(1)}, f32[12,768]{1,0:T(8,128)}, u32[]{:S(2)}) copy-start(f32[12,768]{1,0:T(8,128)} %get-tuple-element.49) | copy-start | bytes 110596
  176.6 258.5 %all-reduce.7.cloned.1.call-start = ((), (), s32[]{:S(2)}) async-start(), calls=%async_computation.3 | async-start | bytes 1572864 | tf_op jit(solution)/shard_map/psum | solution.py:669
Sparse Core Ops, SparseCore 0:
  9.6 40.1 all-gather.7
  51.3 37.4 all-gather.5
  176.7 121.8 all-reduce.4
  304.1 130.8 all-reduce.6

commit v2 on v1

--- a/solution.py
+++ b/solution.py
@@ -13,6 +13,8 @@
 WIDTH = 768
 RANK = 12
 BLOCKS = ROWS // LANES
+TILE = 16
+SPLIT_AT = 25
 
 norm_eps = 1e-07
 masked_fill = -1e30
@@ -115,7 +117,15 @@
     left_t,
     right,
     scale,
+    expand,
+    shrink,
+    expand_right,
+    shrink_left_t,
     shares_out,
+    expand_all,
+    shrink_all,
+    expand_right_all,
+    shrink_left_all,
     q_s,
     k_s,
     v_s,
@@ -127,7 +137,15 @@
     bias_s,
     across_s,
     sems,
+    *gather_sems,
 ):
+    gather = Gather(
+        expand_all.shape[0],
+        (expand, shrink, expand_right, shrink_left_t),
+        (expand_all, shrink_all, expand_right_all, shrink_left_all),
+        gather_sems,
+    )
+    gather.start()
     row, lane = block_iotas()
     below = lane <= row
     flip = (row + lane == LANES - 1).astype(bf16)
@@ -163,6 +181,14 @@
     project(tr_s[...], 1, tk_s)
 
     def pair(p, carry):
+        for k in range(6):
+
+            @pl.when(p == k)
+            def _():
+                gather.forward_one(k)
+                if k:
+                    gather.forward_two(k - 1)
+
         kp = k_s[p]
         tq = tq_s[p]
         tk = tk_s[p]
@@ -198,6 +224,8 @@
         return carry
 
     lax.fori_loop(0, PAIRS, pair, 0)
+    gather.forward_two(5)
+    gather.finish()
 
     def finish(p, carry):
         pltpu.make_async_copy(shares_s.at[p], shares_out.at[p], sems.at[p]).wait()
@@ -210,12 +238,280 @@
     return pl.BlockSpec(memory_space=pltpu.VMEM)
 
 
-def attend(segment, live, tokens, table, mix_weight, left_t, right, scale):
+def anywhere():
+    return pl.BlockSpec(memory_space=pl.ANY)
+
+
+def remote(source, target, send, recv, device):
+    return pltpu.make_async_remote_copy(
+        src_ref=source,
+        dst_ref=target,
+        send_sem=send,
+        recv_sem=recv,
+        device_id=device,
+        device_id_type=pl.DeviceIdType.MESH,
+    )
+
+
+def greet(devices):
+    barrier = pltpu.get_barrier_semaphore()
+    for device in devices:
+        pl.semaphore_signal(
+            barrier, inc=1, device_id=device, device_id_type=pl.DeviceIdType.MESH
+        )
+    pl.semaphore_wait(barrier, len(devices))
+
+
+class Groups:
+    def __init__(self, tensor_size, dp_size):
+        self.near_size = tensor_size * 2
+        self.far_size = dp_size // 2
+        self.tensor = lax.axis_index("tensor")
+        self.dp = lax.axis_index("dp")
+        self.near = self.tensor * 2 + self.dp % 2
+        self.far = self.dp // 2
+
+    def near_index(self, step):
+        return (self.near + step) % self.near_size
+
+    def near_device(self, step):
+        index = self.near_index(step)
+        return {"dp": self.far * 2 + index % 2, "tensor": index // 2}
+
+    def far_device(self, step):
+        index = (self.far + step) % self.far_size
+        return {"dp": index * 2 + self.dp % 2, "tensor": self.tensor}
+
+    def partners(self):
+        return [self.near_device(s) for s in range(1, self.near_size)] + [
+            self.far_device(s) for s in range(1, self.far_size)
+        ]
+
+
+class Reduction:
+    def __init__(self, groups, pack, arrived, crossed, out, sems):
+        self.groups = groups
+        self.pack = pack
+        self.arrived = arrived
+        self.crossed = crossed
+        self.out = out
+        self.send_one, self.recv_one, self.send_two, self.recv_two, self.send_three, self.recv_three = sems
+        self.size = pack.shape[0] // groups.near_size
+
+    def part(self, ref, index):
+        return ref.at[pl.ds(index * self.size, self.size)]
+
+    def scatter(self):
+        g = self.groups
+        return [
+            remote(
+                self.part(self.pack, g.near_index(s)),
+                self.arrived.at[s - 1],
+                self.send_one.at[s - 1],
+                self.recv_one.at[s - 1],
+                g.near_device(s),
+            )
+            for s in range(1, g.near_size)
+        ]
+
+    def cross(self):
+        g = self.groups
+        return [
+            remote(
+                self.crossed.at[g.far],
+                self.crossed.at[g.far],
+                self.send_two.at[s - 1],
+                self.recv_two.at[s - 1],
+                g.far_device(s),
+            )
+            for s in range(1, g.far_size)
+        ]
+
+    def gather(self):
+        g = self.groups
+        return [
+            remote(
+                self.part(self.out, g.near),
+                self.part(self.out, g.near),
+                self.send_three.at[s - 1],
+                self.recv_three.at[s - 1],
+                g.near_device(s),
+            )
+            for s in range(1, g.near_size)
+        ]
+
+    def start(self):
+        for copy in self.scatter():
+            copy.start()
+
+    def middle(self):
+        g = self.groups
+        for copy in self.scatter():
+            copy.wait()
+        total = self.pack[pl.ds(g.near * self.size, self.size)].astype(f32)
+        for s in range(1, g.near_size):
+            total = total + self.arrived[s - 1].astype(f32)
+        self.crossed[g.far] = total.astype(self.crossed.dtype)
+        for copy in self.cross():
+            copy.start()
+
+    def last(self):
+        g = self.groups
+        for copy in self.cross():
+            copy.wait()
+        total = self.crossed[0].astype(f32)
+        for s in range(1, g.far_size):
+            total = total + self.crossed[s].astype(f32)
+        self.out[pl.ds(g.near * self.size, self.size)] = total.astype(self.out.dtype)
+        for copy in self.gather():
+            copy.start()
+
+    def finish(self):
+        for copy in self.gather():
+            copy.wait()
+
+
+def reduction_scratch(tiles, near_size, far_size, kind):
+    size = tiles // near_size
+    near = (near_size - 1,)
+    far = (max(far_size - 1, 1),)
+    dma = pltpu.SemaphoreType.DMA
+    return [
+        pltpu.VMEM((near_size - 1, size, TILE, LANES), kind),
+        pltpu.VMEM((far_size, size, TILE, LANES), kind),
+        dma(near),
+        dma(near),
+        dma(far),
+        dma(far),
+        dma(near),
+        dma(near),
+    ]
+
+
+class Gather:
+    def __init__(self, size, sources, targets, sems):
+        self.size = size
+        self.far = size // 2
+        self.sources = sources
+        self.targets = targets
+        self.across_s, self.across_r, self.pair_s, self.pair_r, self.one_s, self.one_r, self.two_s, self.two_r = sems[:8]
+        self.whole_s, self.whole_r, self.small_s, self.small_r, self.own = sems[8:]
+        self.tensor = lax.axis_index("tensor")
+        self.dp = lax.axis_index("dp")
+        self.bit = self.dp % 2
+        self.pair = {"dp": self.dp + 1 - 2 * self.bit, "tensor": self.tensor}
+        core = self.tensor % 2
+        self.core = {"dp": self.dp, "tensor": self.tensor + 1 - 2 * core}
+
+    def device(self, step):
+        return {"dp": self.dp, "tensor": (self.tensor + step) % self.size}
+
+    def partners(self):
+        return [self.device(s) for s in range(1, self.size)] + [self.pair]
+
+    def rows(self, which, part, bit):
+        count = self.sources[which].shape[0] // 6
+        return pl.ds((2 * part + bit) * count, count)
+
+    def across(self, s, k):
+        which, part = k // 3, k % 3
+        rows = self.rows(which, part, self.bit)
+        return remote(
+            self.sources[which].at[rows, :],
+            self.targets[which].at[self.tensor, rows, :],
+            self.across_s.at[s - 1, k],
+            self.across_r.at[s - 1, k],
+            self.device(2 * s),
+        )
+
+    def onward(self, s, k, bit, sends, recvs, device):
+        which, part = k // 3, k % 3
+        rows = self.rows(which, part, bit)
+        slot = (self.tensor + self.size - 2 * s) % self.size
+        ref = self.targets[which].at[slot, rows, :]
+        return remote(ref, ref, sends.at[s - 1, k], recvs.at[s - 1, k], device)
+
+    def swap(self, s, k):
+        return self.onward(s, k, self.bit, self.pair_s, self.pair_r, self.pair)
+
+    def share_one(self, s, k):
+        return self.onward(s, k, self.bit, self.one_s, self.one_r, self.core)
+
+    def share_two(self, s, k):
+        return self.onward(s, k, 1 - self.bit, self.two_s, self.two_r, self.core)
+
+    def whole(self, which):
+        return remote(
+            self.sources[which],
+            self.targets[which].at[self.tensor],
+            self.whole_s.at[which],
+            self.whole_r.at[which],
+            self.core,
+        )
+
+    def small(self, s, which):
+        return remote(
+            self.sources[which],
+            self.targets[which].at[self.tensor],
+            self.small_s.at[s - 1, which - 2],
+            self.small_r.at[s - 1, which - 2],
+            self.device(s),
+        )
+
+    def keep(self, which):
+        return pltpu.make_async_copy(
+            self.sources[which], self.targets[which].at[self.tensor], self.own.at[which - 2]
+        )
+
+    def start(self):
+        greet(self.partners())
+        for k in range(6):
+            for s in range(1, self.far):
+                self.across(s, k).start()
+        for which in range(2):
+            self.whole(which).start()
+        for s in range(1, self.size):
+            for which in (2, 3):
+                self.small(s, which).start()
+        for which in (2, 3):
+            self.keep(which).start()
+
+    def forward_one(self, k):
+        for s in range(1, self.far):
+            self.across(s, k).wait_recv()
+            self.swap(s, k).start()
+            self.share_one(s, k).start()
+
+    def forward_two(self, k):
+        for s in range(1, self.far):
+            self.swap(s, k).wait_recv()
+            self.share_two(s, k).start()
+
+    def finish(self):
+        for s in range(1, self.far):
+            for k in range(6):
+                self.across(s, k).wait_send()
+                self.swap(s, k).wait_send()
+                self.share_one(s, k).wait()
+                self.share_two(s, k).wait()
+        for which in range(2):
+            self.whole(which).wait()
+        for s in range(1, self.size):
+            for which in (2, 3):
+                self.small(s, which).wait()
+        for which in (2, 3):
+            self.keep(which).wait()
+
+
+def attend(size, *args):
     piece = jax.ShapeDtypeStruct((PAIRS, ROWS, LANES), bf16)
+    dma = pltpu.SemaphoreType.DMA
+    steps = (max(size // 2 - 1, 1), 6)
     return pl.pallas_call(
         attend_kernel,
-        out_shape=(
-            jax.ShapeDtypeStruct((PAIRS, 2, ROWS, ROWS), bf16),
+        out_shape=(jax.ShapeDtypeStruct((PAIRS, 2, ROWS, ROWS), bf16),)
+        + tuple(jax.ShapeDtypeStruct((size,) + array.shape, bf16) for array in args[8:])
+        + (
             piece,
             piece,
             piece,
@@ -224,17 +520,23 @@
             jax.ShapeDtypeStruct((ROWS, WIDTH), bf16),
             piece,
         ),
-        in_specs=[vmem()] * 8,
-        out_specs=(pl.BlockSpec(memory_space=pl.ANY),) + (vmem(),) * 7,
+        in_specs=[vmem()] * 8 + [anywhere()] * 4,
+        out_specs=(anywhere(),) * 5 + (vmem(),) * 7,
         scratch_shapes=[
             pltpu.VMEM((PAIRS, 2, ROWS, ROWS), bf16),
             pltpu.VMEM((ROWS, ROWS), f32),
             pltpu.VMEM((ROWS, ROWS), f32),
-            pltpu.SemaphoreType.DMA((PAIRS,)),
-        ],
-        compiler_params=pltpu.CompilerParams(vmem_limit_bytes=56 * 2**20),
+            dma((PAIRS,)),
+        ]
+        + [dma(steps)] * 8
+        + [dma((2,))] * 2
+        + [dma((size - 1, 2))] * 2
+        + [dma((2,))],
+        compiler_params=pltpu.CompilerParams(
+            vmem_limit_bytes=56 * 2**20, collective_id=0, has_side_effects=True
+        ),
         name="attend",
-    )(segment, live, tokens, table, mix_weight, left_t, right, scale)
+    )(*args)
 
 
 def norm_parts(values):
@@ -268,16 +570,15 @@
     shrink_left_t,
     shrink_right,
     feed_scale,
+    expand_own,
+    shrink_own,
     layer_out,
     grad_first_out,
     grad_context_out,
-    out_left_grad,
-    out_right_grad,
-    expand_left_grad,
-    shrink_right_grad,
-    expand_right_grad,
-    shrink_left_grad,
-    scales_out,
+    pack,
+    expand_s,
+    shrink_s,
+    sems,
     x_s,
     normed_s,
     hidden_s,
@@ -287,6 +588,36 @@
     context_s,
 ):
     chunks = expand.shape[0]
+    pieces = expand.shape[2] // LANES
+
+    def loads(c):
+        return (
+            pltpu.make_async_copy(expand.at[c], expand_s.at[c], sems.at[0, c]),
+            pltpu.make_async_copy(shrink.at[c], shrink_s.at[c], sems.at[1, c]),
+        )
+
+    me = lax.axis_index("tensor")
+
+    def begin(c, carry):
+        @pl.when(c == me)
+        def _():
+            pltpu.make_async_copy(expand_own, expand_s.at[c], sems.at[0, c]).start()
+            pltpu.make_async_copy(shrink_own, shrink_s.at[c], sems.at[1, c]).start()
+
+        @pl.when(c != me)
+        def _():
+            for copy in loads(c):
+                copy.start()
+
+        return carry
+
+    lax.fori_loop(0, chunks, begin, 0)
+    pack[...] = jnp.zeros_like(pack)
+
+    def keep(first, values):
+        for j in range(values.shape[1] // LANES):
+            pack[first + j, :RANK, :] = values[:, j * LANES : (j + 1) * LANES]
+
     wide = lax.broadcasted_iota(jnp.int32, (RANK, LANES), 1)
     lam_out = column_of(scale[3:4, :])
     lam_one = column_of(feed_scale[0:1, :])
@@ -317,12 +648,14 @@
     branch_s[...] = jnp.zeros_like(branch_s)
 
     def forward(c, two_rank):
-        pre = dot_nn(hidden_s[...], expand[c]) + dot_tn(one_low, expand_right[c])
+        for copy in loads(c):
+            copy.wait()
+        pre = dot_nn(hidden_s[...], expand_s[c]) + dot_tn(one_low, expand_right[c])
         cdf = 0.5 + 0.5 * lax.erf(pre * inverse_root_two)
         act = (pre * cdf).astype(bf16)
         act_s[c] = act
         slope_s[c] = cdf + pre * jnp.exp(-0.5 * pre * pre) * inverse_root_tau
-        branch_s[...] += dot_nn(act, shrink[c])
+        branch_s[...] += dot_nn(act, shrink_s[c])
         return two_rank + dot_nt(shrink_left_t[c], act)
 
     two_rank = lax.fori_loop(0, chunks, forward, jnp.zeros((RANK, ROWS), f32))
@@ -341,21 +674,21 @@
     grad_branch = branch_s[...].astype(bf16)
     two_back = dot_nt(shrink_right[...], grad_branch)
     two_small = (two_back * lam_two).astype(bf16)
-    shrink_right_grad[...] = dot_nn(two_low, grad_branch)
+    keep(18, dot_nn(two_low, grad_branch))
     two_scale = jnp.sum(two_rank * two_back, axis=1, keepdims=True)
 
     def backward(c, one_back):
-        grad_act = dot_nt(grad_branch, shrink[c]) + dot_tn(two_small, shrink_left_t[c])
+        grad_act = dot_nt(grad_branch, shrink_s[c]) + dot_tn(two_small, shrink_left_t[c])
         grad_pre = (grad_act * slope_s[c]).astype(bf16)
-        shrink_left_grad[c] = dot_nn(two_small, act_s[c])
-        expand_right_grad[c] = dot_nn(one_low, grad_pre)
-        branch_s[...] += dot_nt(grad_pre, expand[c])
+        keep(SPLIT_AT + (chunks + c) * pieces, dot_nn(two_small, act_s[c]))
+        keep(SPLIT_AT + c * pieces, dot_nn(one_low, grad_pre))
+        branch_s[...] += dot_nt(grad_pre, expand_s[c])
         return one_back + dot_nt(expand_right[c], grad_pre)
 
     one_back = lax.fori_loop(0, chunks, backward, jnp.zeros((RANK, ROWS), f32))
     one_small = (one_back * lam_one).astype(bf16)
     branch_s[...] += dot_tn(one_small, expand_left_t[...])
-    expand_left_grad[...] = dot_nn(one_small, hidden_s[...])
+    keep(12, dot_nn(one_small, hidden_s[...]))
     one_scale = jnp.sum(one_rank * one_back, axis=1, keepdims=True)
 
     def first_back(i, carry):
@@ -368,40 +701,39 @@
     grad_attended = grad_first_out[...].astype(bf16)
     out_back = dot_nt(right[:, 3, :], grad_attended)
     out_small = (out_back * lam_out).astype(bf16)
-    grad_context_out[...] = (
-        dot_nt(grad_attended, out_weight[...]) + dot_tn(out_small, left_t[:, 3, :])
-    ).astype(bf16)
-    out_left_grad[...] = dot_nn(out_small, context_s[...])
-    out_right_grad[...] = dot_nn(out_low, grad_attended)
+    grad_context = dot_nt(grad_attended, out_weight[...]) + dot_tn(out_small, left_t[:, 3, :])
+    for p in range(PAIRS):
+        grad_context_out[p] = grad_context[:, p * LANES : (p + 1) * LANES].astype(bf16)
+    keep(0, dot_nn(out_small, context_s[...]))
+    keep(6, dot_nn(out_low, grad_attended))
     out_scale = jnp.sum(out_rank * out_back, axis=1, keepdims=True)
-    scales_out[...] = jnp.where(
-        wide == 3,
-        out_scale,
-        jnp.where(wide == 4, one_scale, jnp.where(wide == 5, two_scale, 0.0)),
+    keep(
+        24,
+        jnp.where(
+            wide == 3,
+            out_scale,
+            jnp.where(wide == 4, one_scale, jnp.where(wide == 5, two_scale, 0.0)),
+        ),
     )
 
 
-def feed(*args):
+def feed(tiles, *args):
     chunks, _, hidden = args[9].shape
-    small = jax.ShapeDtypeStruct((RANK, WIDTH), f32)
-    parts = jax.ShapeDtypeStruct((chunks, RANK, hidden), f32)
     return pl.pallas_call(
         feed_kernel,
         out_shape=(
             jax.ShapeDtypeStruct((ROWS, WIDTH), bf16),
             jax.ShapeDtypeStruct((ROWS, WIDTH), f32),
-            jax.ShapeDtypeStruct((ROWS, WIDTH), bf16),
-            small,
-            small,
-            small,
-            small,
-            parts,
-            parts,
-            jax.ShapeDtypeStruct((RANK, LANES), f32),
+            jax.ShapeDtypeStruct((PAIRS, ROWS, LANES), bf16),
+            jax.ShapeDtypeStruct((tiles, TILE, LANES), f32),
         ),
-        in_specs=[vmem()] * 16,
-        out_specs=(vmem(),) * 10,
+        in_specs=[vmem()] * 9
+        + [anywhere(), vmem(), vmem(), anywhere(), vmem(), vmem(), vmem(), anywhere(), anywhere()],
+        out_specs=(vmem(),) * 4,
         scratch_shapes=[
+            pltpu.VMEM((chunks, WIDTH, hidden), bf16),
+            pltpu.VMEM((chunks, hidden, WIDTH), bf16),
+            pltpu.SemaphoreType.DMA((2, chunks)),
             pltpu.VMEM((ROWS, WIDTH), f32),
             pltpu.VMEM((ROWS, WIDTH), f32),
             pltpu.VMEM((ROWS, WIDTH), bf16),
@@ -430,10 +762,10 @@
     left_t,
     right,
     scale,
+    early,
     grad_tokens,
-    left_grad,
-    right_grad,
-    scales_out,
+    early_out,
+    tail_out,
     shares_s,
     gl_s,
     qf_s,
@@ -445,8 +777,14 @@
     gv_t,
     gtq_t,
     gtk_t,
+    tail,
     sems,
+    *reduce_refs,
 ):
+    arrived, crossed = reduce_refs[0], reduce_refs[1]
+    groups = Groups(arrived.shape[0] // 2 + 1, crossed.shape[0] * 2)
+    first = Reduction(groups, early, arrived, crossed, early_out, reduce_refs[2:8])
+    second = Reduction(groups, tail, reduce_refs[8], reduce_refs[9], tail_out, reduce_refs[10:16])
     row, lane = block_iotas()
     below_rev = lane + row <= LANES - 1
     lane_first = lane == 0
@@ -458,6 +796,13 @@
         return carry
 
     lax.fori_loop(0, PAIRS, begin, 0)
+    greet(groups.partners())
+    first.start()
+    tail[...] = jnp.zeros_like(tail)
+
+    def keep(index, values):
+        for j in range(values.shape[1] // LANES):
+            tail[index + j, :RANK, :] = values[:, j * LANES : (j + 1) * LANES].astype(bf16)
 
     def flipped(values):
         return jnp.concatenate(
@@ -470,6 +815,15 @@
 
     def pair(p, carry):
         pltpu.make_async_copy(shares_in.at[p], shares_s.at[p], sems.at[p]).wait()
+
+        @pl.when(p == 2)
+        def _():
+            first.middle()
+
+        @pl.when(p == 4)
+        def _():
+            first.last()
+
         gc = grad_context[p]
         gc_t = gc.T
         q_rev_t = flipped(q_s[p]).T
@@ -515,10 +869,12 @@
 
     lax.fori_loop(0, PAIRS, pair, 0)
 
+    first.finish()
     wide = lax.broadcasted_iota(jnp.int32, (RANK, LANES), 1)
-    total = grad_first[...]
     scales = jnp.zeros((RANK, LANES), f32)
     source = tokens[...]
+    grads = []
+    smalls = []
     for which in range(3):
         if which == 2:
             grad = gv_t[...].T
@@ -530,7 +886,8 @@
         low = (rank * lam).astype(bf16)
         back = dot_nt(right[:, which, :], grad)
         small = (back * lam).astype(bf16)
-        total = total + dot_nt(grad, mix_weight[which]) + dot_tn(small, left)
+        grads.append(grad)
+        smalls.append(small)
         left_sum = dot_nn(small, source)
         right_sum = dot_nn(low, grad)
         scale_sum = jnp.sum(rank * back, axis=1, keepdims=True)
@@ -543,25 +900,37 @@
             left_sum = left_sum + dot_nn(small, tr_s[...])
             right_sum = right_sum + dot_nt(low, table_grad)
             scale_sum = scale_sum + jnp.sum(rank * back, axis=1, keepdims=True)
-        left_grad[which] = left_sum
-        right_grad[which] = right_sum
+        keep(which * 6, left_sum)
+        keep(18 + which * 6, right_sum)
         scales = jnp.where(wide == which, scale_sum, scales)
+    keep(36, scales)
+    second.start()
+    total = grad_first[...]
+    for which in range(3):
+        if which == 1:
+            second.middle()
+        if which == 2:
+            second.last()
+        total = (
+            total
+            + dot_nt(grads[which], mix_weight[which])
+            + dot_tn(smalls[which], left_t[:, which, :])
+        )
     grad_tokens[...] = total
-    scales_out[...] = scales
-
-
-def back(*args):
-    sums = jax.ShapeDtypeStruct((3, RANK, WIDTH), f32)
+    second.finish()
+
+
+def back(tail_tiles, near_size, far_size, *args):
+    early = args[-1]
     return pl.pallas_call(
         back_kernel,
         out_shape=(
             jax.ShapeDtypeStruct((ROWS, WIDTH), f32),
-            sums,
-            sums,
-            jax.ShapeDtypeStruct((RANK, LANES), f32),
+            jax.ShapeDtypeStruct(early.shape, f32),
+            jax.ShapeDtypeStruct((tail_tiles, TILE, LANES), bf16),
         ),
-        in_specs=[vmem(), vmem(), pl.BlockSpec(memory_space=pl.ANY)] + [vmem()] * 11,
-        out_specs=(vmem(),) * 4,
+        in_specs=[vmem(), vmem(), anywhere()] + [vmem()] * 12,
+        out_specs=(vmem(),) * 3,
         scratch_shapes=[
             pltpu.VMEM((PAIRS, 2, ROWS, ROWS), bf16),
             pltpu.VMEM((ROWS, ROWS), bf16),
@@ -574,11 +943,82 @@
             pltpu.VMEM((WIDTH, ROWS), bf16),
             pltpu.VMEM((WIDTH, ROWS), bf16),
             pltpu.VMEM((WIDTH, ROWS), bf16),
+            pltpu.VMEM((tail_tiles, TILE, LANES), bf16),
             pltpu.SemaphoreType.DMA((PAIRS,)),
-        ],
-        compiler_params=pltpu.CompilerParams(vmem_limit_bytes=58 * 2**20),
+        ]
+        + reduction_scratch(early.shape[0], near_size, far_size, f32)
+        + reduction_scratch(tail_tiles, near_size, far_size, bf16),
+        compiler_params=pltpu.CompilerParams(
+            vmem_limit_bytes=58 * 2**20, collective_id=1, has_side_effects=True
+        ),
         name="back",
     )(*args)
+
+
+def unpack_kernel(
+    early,
+    tail,
+    tokens_in,
+    tokens_out,
+    left,
+    scale,
+    right,
+    expand_left_t,
+    expand_right,
+    shrink_left_t,
+    feed_scale,
+    shrink_right,
+    sem,
+):
+    copy = pltpu.make_async_copy(tokens_in, tokens_out, sem)
+    copy.start()
+    me = lax.axis_index("tensor")
+    pieces = expand_right.shape[1] // LANES
+    split = SPLIT_AT + me * pieces
+    skip = (early.shape[0] - SPLIT_AT) // 2
+    for j in range(WIDTH // LANES):
+        lanes = slice(j * LANES, (j + 1) * LANES)
+        for which in range(3):
+            left[:, which, lanes] = tail[which * 6 + j, :RANK, :].astype(f32)
+            right[:, which, lanes] = tail[18 + which * 6 + j, :RANK, :].astype(f32)
+        left[:, 3, lanes] = early[j, :RANK, :]
+        right[:, 3, lanes] = early[6 + j, :RANK, :]
+        expand_left_t[:, lanes] = early[12 + j, :RANK, :]
+        shrink_right[:, lanes] = early[18 + j, :RANK, :]
+    total = lax.axis_size("tensor") * pieces
+    for j in range(pieces):
+        lanes = slice(j * LANES, (j + 1) * LANES)
+        expand_right[:, lanes] = early[split + j, :RANK, :]
+        shrink_left_t[:, lanes] = early[split + total + j, :RANK, :]
+    wide = lax.broadcasted_iota(jnp.int32, (TILE, LANES), 1)
+    both = jnp.where(wide < 3, tail[36].astype(f32), early[24]).T
+    scale[...] = both[:4, :RANK]
+    feed_scale[...] = both[4:6, :RANK]
+    copy.wait()
+
+
+def unpack(hidden, early, tail, tokens):
+    mats = jax.ShapeDtypeStruct((RANK, 4, WIDTH), f32)
+    small = jax.ShapeDtypeStruct((RANK, WIDTH), f32)
+    split = jax.ShapeDtypeStruct((RANK, hidden), f32)
+    return pl.pallas_call(
+        unpack_kernel,
+        out_shape=(
+            jax.ShapeDtypeStruct((ROWS, WIDTH), f32),
+            mats,
+            jax.ShapeDtypeStruct((4, RANK), f32),
+            mats,
+            small,
+            split,
+            split,
+            jax.ShapeDtypeStruct((2, RANK), f32),
+            small,
+        ),
+        in_specs=[vmem(), vmem(), vmem()],
+        out_specs=(anywhere(),) + (vmem(),) * 8,
+        scratch_shapes=[pltpu.SemaphoreType.DMA],
+        name="unpack",
+    )(early, tail, tokens)
 
 
 def body(
@@ -602,12 +1042,29 @@
     shrink_right,
     cotangent,
 ):
+    tensor_size = lax.axis_size("tensor")
+    near_size = tensor_size * 2
+    far_size = lax.axis_size("dp") // 2
+    hidden = expand_weight.shape[1]
+    early_tiles = -(-(SPLIT_AT + 2 * tensor_size * hidden // LANES) // near_size) * near_size
+    tail_tiles = -(-37 // near_size) * near_size
     left_t = jnp.transpose(mix_left, (2, 0, 1))
     right = jnp.transpose(mix_right, (1, 0, 2))
-    expand_all = lax.all_gather(expand_weight, "tensor")
-    shrink_all = lax.all_gather(shrink_weight, "tensor")
-    small_all = lax.all_gather(jnp.stack([expand_right, shrink_left.T]), "tensor")
-    shares, q, k, v, tq, tk, tr, context = attend(
+    (
+        shares,
+        expand_all,
+        shrink_all,
+        expand_right_all,
+        shrink_left_all,
+        q,
+        k,
+        v,
+        tq,
+        tk,
+        tr,
+        context,
+    ) = attend(
+        tensor_size,
         segment.reshape(1, ROWS),
         live.reshape(1, ROWS),
         tokens,
@@ -616,19 +1073,13 @@
         left_t,
         right,
         mix_scale,
+        expand_weight,
+        shrink_weight,
+        expand_right,
+        shrink_left.T,
     )
-    (
-        layer_out,
-        grad_first,
-        grad_context,
-        out_left_g,
-        out_right_g,
-        expand_left_g,
-        shrink_right_g,
-        expand_right_g,
-        shrink_left_g,
-        feed_scales,
-    ) = feed(
+    layer_out, grad_first, grad_context, early = feed(
+        early_tiles,
         context,
         tokens,
         cotangent,
@@ -640,15 +1091,19 @@
         norm_bias,
         expand_all,
         expand_left.T,
-        small_all[:, 0],
+        expand_right_all,
         shrink_all,
-        small_all[:, 1],
+        shrink_left_all,
         shrink_right,
         feed_scale,
+        expand_weight,
+        shrink_weight,
     )
-    grad_pieces = jnp.transpose(grad_context.reshape(ROWS, PAIRS, LANES), (1, 0, 2))
-    grad_tokens, left_g, right_g, mix_scales = back(
-        grad_pieces,
+    grad_tokens, early, tail = back(
+        tail_tiles,
+        near_size,
+        far_size,
+        grad_context,
         grad_first,
         shares,
         q,
@@ -662,34 +1117,22 @@
         left_t,
         right,
         mix_scale,
+        early,
     )
-    left_g = jnp.concatenate([left_g, out_left_g[None]])
-    right_g = jnp.concatenate([right_g, out_right_g[None]])
-    scales = feed_scales + mix_scales
-    left_g, right_g, scales, expand_left_g, shrink_right_g, expand_right_g, shrink_left_g = lax.psum(
-        (
-            left_g,
-            right_g,
-            scales,
-            expand_left_g,
-            shrink_right_g,
-            expand_right_g,
-            shrink_left_g,
-        ),
-        ("dp", "tensor"),
+    grad_tokens, left, scale, right, expand_left, expand_right, shrink_left, feed_scale, shrink_right = unpack(
+        hidden, early, tail, grad_tokens
     )
-    me = lax.axis_index("tensor")
     return (
         layer_out,
         grad_tokens,
-        jnp.transpose(left_g, (0, 2, 1)),
-        scales[:, :4].T,
-        right_g,
-        expand_left_g.T,
-        lax.dynamic_index_in_dim(expand_right_g, me, 0, keepdims=False),
-        lax.dynamic_index_in_dim(shrink_left_g, me, 0, keepdims=False).T,
-        scales[:, 4:6].T,
-        shrink_right_g,
+        jnp.transpose(left, (1, 2, 0)),
+        scale,
+        jnp.transpose(right, (1, 0, 2)),
+        expand_left.T,
+        expand_right,
+        shrink_left.T,
+        feed_scale,
+        shrink_right,
     )
 
 

time: 451 us -> 146 us (0.32)
  waiting for transfers between devices: 288 us -> 0 us
  Pallas kernels: 123 us -> 145 us
  local copies, waits for them, and re-layouts: 15.1 us -> 0 us
  between operations: 13.9 us -> 0.85 us
  blocking collectives: 6.87 us -> 0 us
    psum x2 -> x0, waiting for transfers between devices: 254 us -> none  [body(): lax.psum((left_g, right_g, scales, expand_left_g, shrink_right_g, expand_...]
    all_gather x2 -> x0, waiting for transfers between devices: 32.9 us -> none  [the longest x1 32.9 us: body(): expand_all = lax.all_gather(expand_weight, 'tensor')]
    pallas_call x1, Pallas kernels: 51.4 us -> 63.2 us  [back(): pl.pallas_call(back_kernel, out_shape=(jax.ShapeDtypeStruct((ROWS, WIDTH)...]
    pallas_call x1, Pallas kernels: 39.6 us -> 49.1 us  [attend(): pl.pallas_call(attend_kernel, out_shape=(jax.ShapeDtypeStruct((PAIRS, 2,...]
    unnamed x16 -> x0, local copies, waits for them, and re-layouts: 7.54 us -> none
    all_gather x1 -> x0, blocking collectives: 6.87 us -> none  [body(): lax.all_gather(jnp.stack([expand_right, shrink_left.T]), 'tensor')]
  transfers between devices with their start and end apart: 4 -> 0, of which waited for: 3 -> 0; matrix products, arithmetic and copies ran while one was open for 1% -> 0% of each run, Pallas kernels for 9% -> 0%
where the time goes in v2:
time: 146 us
  Pallas kernels  145 us (99%)
    pallas_call x1, Pallas kernels, back(): pl.pallas_call(back_kernel, out_shape=(jax.ShapeDtypeStruct((ROWS, WIDTH)...  63.2 us
    pallas_call x1, Pallas kernels, attend(): pl.pallas_call(attend_kernel, out_shape=(jax.ShapeDtypeStruct((PAIRS, 2,...  49.1 us
    pallas_call x1, Pallas kernels, feed(): pl.pallas_call(feed_kernel, out_shape=(jax.ShapeDtypeStruct((ROWS, WIDTH)...  29.3 us
    pallas_call x1, Pallas kernels, unpack(): pl.pallas_call(unpack_kernel, out_shape=(jax.ShapeDtypeStruct((ROWS, WIDT...  3.63 us

profile of v2, /device:TPU:0, one launch (start us, length us, event | category | flops | bytes accessed | tf_op | source)
XLA Modules:
  0.0 146.2 jit_solution(8926069887275158267)
XLA Ops:
  0.6 49.1 %attend.1 = (bf16[6,2,512,512]{3,2,1,0:T(8,128)(2,1)}, bf16[4,768,768]{2,1,0:T(8,128)(2,1)}, bf16[4,768,768]{2,1,0:T(8,128)(2,1)}, bf16[4,12,768]{2,1,0:T(8,128)...) custom-call(s32[1,512]{1,0:T(1,128)} %bitcast.18, ...), custom_call_target="tpu_custom_call" | custom-call | tf_op jit(solution)/shard_map/attend/pallas_call | solution.py:510
  49.8 29.3 %feed.1 = (bf16[512,768]{1,0:T(8,128)(2,1)}, f32[512,768]{1,0:T(8,128)}, bf16[6,512,128]{2,1,0:T(8,128)(2,1)}, f32[80,16,128]{2,1,0:T(8,128)}) custom-call(bf16[6,512,128]{2,1,0:T(8,128)(2,1)} %get-tuple-element.38.context, bf16[512,768]{1,0:T(8,128)(2,1)} %tokens.5, bf16[512,768]{1,0:T(8,128)(2,1)} %cotangent.1, bf16[768,768]{1,0:T(8,128)(2,1)} %out_weight.1, ...), custom_call_target="tpu_custom_call" | custom-call | tf_op jit(solution)/shard_map/feed/pallas_call | solution.py:722
  79.1 63.2 %back.1 = (f32[512,768]{1,0:T(8,128)}, f32[80,16,128]{2,1,0:T(8,128)}, bf16[40,16,128]{2,1,0:T(8,128)(2,1)}) custom-call(bf16[6,512,128]{2,1,0:T(8,128)(2,1)} %get-tuple-element.44.grad_context, f32[512,768]{1,0:T(8,128)} %get-tuple-element.45.grad_first, bf16[6,2,512,512]{3,2,1,0:T(8,128)(2,1)} %get-tuple-element.46.shares_in, ...), custom_call_target="tpu_custom_call" | custom-call | tf_op jit(solution)/shard_map/back/pallas_call | solution.py:925
  142.4 3.6 %unpack.1 = (f32[512,768]{1,0:T(8,128)}, f32[12,4,768]{2,1,0:T(4,128)}, f32[4,12]{1,0:T(4,128)}, f32[12,4,768]{2,1,0:T(4,128)}, f32[12,768]{1,0:T(8,128)}, /*ind...) custom-call(f32[80,16,128]{2,1,0:T(8,128)} %get-tuple-element.54.early, ...), custom_call_target="tpu_custom_call" | custom-call | tf_op jit(solution)/shard_map/unpack/pallas_call | solution.py:1004

commit v3 on v2

v3 whole, which is shorter than its diff:
```python
import math

import jax
import jax.numpy as jnp
from jax import lax
from jax.experimental import pallas as pl
from jax.experimental.pallas import tpu as pltpu
from jax.sharding import PartitionSpec as P

PAIRS = 6
LANES = 128
ROWS = 512
WIDTH = 768
RANK = 12
BLOCKS = ROWS // LANES
TILE = 16
GROUP = 2
BACK_GROUP = 4
STACK = 64
SPLIT_AT = 25

norm_eps = 1e-07
masked_fill = -1e30
score_scale = 1.0 / math.sqrt(192.0)
inverse_root_two = 1.0 / math.sqrt(2.0)
log_two_e = math.log2(math.e)
inverse_root_tau = 1.0 / math.sqrt(2.0 * math.pi)

f32 = jnp.float32
bf16 = jnp.bfloat16


def dot_nn(left, right):
    return jnp.dot(left, right, preferred_element_type=f32)


def dot_nt(left, right):
    return lax.dot_general(left, right, (((1,), (1,)), ((), ())), preferred_element_type=f32)


def dot_tn(left, right):
    return lax.dot_general(left, right, (((0,), (0,)), ((), ())), preferred_element_type=f32)


def column_of(row):
    n = row.shape[1]
    eye = lax.broadcasted_iota(jnp.int32, (n, n), 0) == lax.broadcasted_iota(jnp.int32, (n, n), 1)
    return jnp.sum(jnp.where(eye, row, 0.0), axis=1, keepdims=True)


def spread(scale):
    row = lax.broadcasted_iota(jnp.int32, (RANK, STACK), 0)
    lane = lax.broadcasted_iota(jnp.int32, (RANK, STACK), 1)
    total = jnp.zeros((1, STACK), f32)
    for a in range(4):
        column = column_of(scale[a : a + 1, :])
        total = total + jnp.sum(
            jnp.where(lane == row + TILE * a, column, 0.0), axis=0, keepdims=True
        )
    return total


def of_map(which):
    lane = lax.broadcasted_iota(jnp.int32, (1, STACK), 1)
    return (lane // TILE == which).astype(bf16)


def block_iotas():
    shape = (LANES, LANES)
    return lax.broadcasted_iota(jnp.int32, shape, 0), lax.broadcasted_iota(jnp.int32, shape, 1)


def head_mask(which):
    lane = lax.broadcasted_iota(jnp.int32, (1, LANES), 1)
    return ((lane >= 64) if which else (lane < 64)).astype(bf16)


def pick_tiles(scores, block, at_diag):
    first = scores[:, :1]
    last = scores[:, ROWS - 1 :]
    near = {}

    def rolled(u):
        if u not in near:
            near[u] = pltpu.roll(
                scores[:, u * LANES : (u + 1) * LANES], 1, 1, stride=1, stride_axis=0
            )
        return near[u]

    tiles = []
    for other in range(BLOCKS):
        v = other - block + 2
        if v < 0:
            tile = jnp.broadcast_to(first, (LANES, LANES))
        elif v == 0:
            tile = jnp.where(at_diag, first, rolled(0))
        elif v < 4:
            tile = jnp.where(at_diag, rolled(v - 1), rolled(v))
        elif v == 4:
            tile = jnp.where(at_diag, rolled(3), last)
        else:
            tile = jnp.broadcast_to(last, (LANES, LANES))
        tiles.append(tile)
    return tiles


def row_sums(values):
    part = (
        values[:, :LANES]
        + values[:, LANES : 2 * LANES]
        + values[:, 2 * LANES : 3 * LANES]
        + values[:, 3 * LANES :]
    )
    high = part.astype(bf16)
    rest = (part - high.astype(f32)).astype(bf16)
    return dot_nn(jnp.concatenate([high, rest], axis=1), jnp.ones((2 * LANES, LANES), bf16))


def wide4(values):
    return jnp.concatenate([values] * BLOCKS, axis=1)


def fold_rows(grads, block, beyond, inside, pick_first, pick_last):
    zero = jnp.zeros((LANES, LANES), f32)
    near = {}
    low = []
    high = []
    for other in range(BLOCKS):
        v = other - block + 2
        tile = grads[:, other * LANES : (other + 1) * LANES]
        if v < 0:
            low.append(tile.astype(bf16))
        elif v > 4:
            high.append(tile.astype(bf16))
        else:
            near[v] = pltpu.roll(tile, 0, 1, stride=1, stride_axis=0)
        if v == 0:
            low.append(tile.astype(bf16) * inside)
        if v == 4:
            high.append(tile.astype(bf16) * (1 - inside))
    out = []
    for w in range(BLOCKS):
        if w in near or w + 1 in near:
            out.append(jnp.where(beyond, near.get(w + 1, zero), near.get(w, zero)))
        else:
            out.append(zero)
    if low:
        out[0] = out[0] + dot_nn(
            jnp.concatenate(low, axis=1), pick_first[: LANES * len(low), :]
        )
    if high:
        out[3] = out[3] + dot_nn(
            jnp.concatenate(high, axis=1), pick_last[: LANES * len(high), :]
        )
    return jnp.concatenate(out, axis=1)


def attend_part(
    segment,
    live,
    tokens,
    table,
    mix_weight,
    mix_copies,
    left_s,
    right_s,
    scale_row,
    rank_s,
    table_rank_s,
    shares_out,
    q_s,
    k_s,
    v_s,
    tq_s,
    tk_s,
    tr_s,
    context_s,
    shares_s,
    bias_s,
    across_s,
    sems,
    gather,
):
    row, lane = block_iotas()
    below = lane <= row
    flip = (row + lane == LANES - 1).astype(bf16)
    eye = (row == lane).astype(bf16)
    seg_row = segment[...]
    key_row = jnp.where(live[...] == 1, seg_row, -1)
    for a in range(BLOCKS):
        seg_col = jnp.broadcast_to(
            seg_row[:, a * LANES : (a + 1) * LANES].astype(f32), (LANES, LANES)
        ).T.astype(jnp.int32)
        for b in range(BLOCKS):
            same = seg_col == key_row[:, b * LANES : (b + 1) * LANES]
            if a == b:
                same = same | (row == lane)
            bias_s[a * LANES : (a + 1) * LANES, b * LANES : (b + 1) * LANES] = jnp.where(
                same, 0.0, masked_fill
            )
    for a in range(BLOCKS):
        tr_s[a * LANES : (a + 1) * LANES, :] = dot_nn(
            flip, table[(3 - a) * LANES : (4 - a) * LANES, :]
        ).astype(bf16)

    rank_s[...] = dot_nt(tokens[...], left_s[...])
    table_rank_s[...] = dot_nt(tr_s[...], left_s[...])
    low = (rank_s[...] * scale_row).astype(bf16)
    table_low = (table_rank_s[...] * scale_row).astype(bf16)

    def project(source, low, which, target):
        full = dot_nn(source, mix_weight[which]) + dot_nn(low * of_map(which), right_s[...])
        for p in range(PAIRS):
            target[p] = full[:, p * LANES : (p + 1) * LANES].astype(bf16)

    mix_copies[0].wait()
    project(tokens[...], low, 0, q_s)
    project(tr_s[...], table_low, 0, tq_s)
    mix_copies[1].wait()
    project(tokens[...], low, 1, k_s)
    project(tr_s[...], table_low, 1, tk_s)
    gather.forward_one(0)
    mix_copies[2].wait()
    project(tokens[...], low, 2, v_s)

    def key_side(p, which, group):
        top = group * GROUP * LANES
        scores = dot_nt(
            k_s[p, top : top + GROUP * LANES, :] * head_mask(which), tq_s[p]
        )
        for i in range(GROUP):
            tiles = pick_tiles(
                scores[i * LANES : (i + 1) * LANES, :], group * GROUP + i, below
            )
            across_s[which, top + i * LANES : top + (i + 1) * LANES, :] = jnp.concatenate(
                tiles, axis=1
            ).astype(bf16)

    def query_side(p, which, group):
        mask = head_mask(which)
        blocks = range(group * GROUP, (group + 1) * GROUP)
        rows = [slice(a * LANES, (a + 1) * LANES) for a in blocks]
        every = slice(rows[0].start, rows[-1].stop)
        queries = [q_s[p, r, :] * mask for r in rows]
        scores = dot_nt(q_s[p, every, :] * mask, tk_s[p])
        totals = [
            dot_nt(
                jnp.concatenate([q, eye], axis=1),
                jnp.concatenate([k_s[p], across_s[which, :, r]], axis=1),
            )
            for q, r in zip(queries, rows)
        ]
        totals = [
            t
            + jnp.concatenate(
                pick_tiles(scores[i * LANES : (i + 1) * LANES, :], blocks[i], below), axis=1
            )
            + bias_s[rows[i], :]
            for i, t in enumerate(totals)
        ]
        peaks = [jnp.max(t, axis=1, keepdims=True) for t in totals]
        weights = [
            jnp.exp2((t - m) * (score_scale * log_two_e)) for t, m in zip(totals, peaks)
        ]
        inverses = [1.0 / jnp.sum(w, axis=1, keepdims=True) for w in weights]
        for r, w, inverse in zip(rows, weights, inverses):
            shares_s[p, which, r, :] = (w * inverse).astype(bf16)
        return dot_nn(shares_s[p, which, every, :], v_s[p] * mask)

    groups = BLOCKS // GROUP
    for group in range(groups):
        key_side(0, 0, group)

    def pair(p, carry):
        for k in range(6):

            @pl.when(p == k)
            def _():
                if k:
                    gather.forward_one(k)
                if k > 1:
                    gather.forward_two(k - 2)

        later = jnp.minimum(p + 1, PAIRS - 1)
        context = []
        for group in range(groups):
            context.append(query_side(p, 0, group))
            key_side(p, 1, group)
        for group in range(groups):
            part = context[group] + query_side(p, 1, group)
            context_s[
                group * GROUP * LANES : (group + 1) * GROUP * LANES,
                pl.ds(pl.multiple_of(p * LANES, LANES), LANES),
            ] = part.astype(bf16)
            key_side(later, 0, group)
        pltpu.make_async_copy(shares_s.at[p], shares_out.at[p], sems.at[p]).start()
        return carry

    lax.fori_loop(0, PAIRS, pair, 0)
    gather.forward_two(4)


def vmem():
    return pl.BlockSpec(memory_space=pltpu.VMEM)


def anywhere():
    return pl.BlockSpec(memory_space=pl.ANY)


def remote(source, target, send, recv, device):
    return pltpu.make_async_remote_copy(
        src_ref=source,
        dst_ref=target,
        send_sem=send,
        recv_sem=recv,
        device_id=device,
        device_id_type=pl.DeviceIdType.MESH,
    )


def greet(devices):
    barrier = pltpu.get_barrier_semaphore()
    for device in devices:
        pl.semaphore_signal(
            barrier, inc=1, device_id=device, device_id_type=pl.DeviceIdType.MESH
        )
    pl.semaphore_wait(barrier, len(devices))


class Groups:
    def __init__(self, tensor_size, dp_size):
        self.near_size = tensor_size * 2
        self.far_size = dp_size // 2
        self.tensor = lax.axis_index("tensor")
        self.dp = lax.axis_index("dp")
        self.near = self.tensor * 2 + self.dp % 2
        self.far = self.dp // 2

    def near_index(self, step):
        return (self.near + step) % self.near_size

    def near_device(self, step):
        index = self.near_index(step)
        return {"dp": self.far * 2 + index % 2, "tensor": index // 2}

    def far_device(self, step):
        index = (self.far + step) % self.far_size
        return {"dp": index * 2 + self.dp % 2, "tensor": self.tensor}

    def partners(self):
        return [self.near_device(s) for s in range(1, self.near_size)] + [
            self.far_device(s) for s in range(1, self.far_size)
        ]


class Reduction:
    def __init__(self, groups, pack, arrived, crossed, out, sems):
        self.groups = groups
        self.pack = pack
        self.arrived = arrived
        self.crossed = crossed
        self.out = out
        self.send_one, self.recv_one, self.send_two, self.recv_two, self.send_three, self.recv_three = sems
        self.size = pack.shape[0] // groups.near_size

    def part(self, ref, index):
        return ref.at[pl.ds(index * self.size, self.size)]

    def scatter(self):
        g = self.groups
        return [
            remote(
                self.part(self.pack, g.near_index(s)),
                self.arrived.at[s - 1],
                self.send_one.at[s - 1],
                self.recv_one.at[s - 1],
                g.near_device(s),
            )
            for s in range(1, g.near_size)
        ]

    def cross(self):
        g = self.groups
        return [
            remote(
                self.crossed.at[g.far],
                self.crossed.at[g.far],
                self.send_two.at[s - 1],
                self.recv_two.at[s - 1],
                g.far_device(s),
            )
            for s in range(1, g.far_size)
        ]

    def gather(self):
        g = self.groups
        return [
            remote(
                self.part(self.out, g.near),
                self.part(self.out, g.near),
                self.send_three.at[s - 1],
                self.recv_three.at[s - 1],
                g.near_device(s),
            )
            for s in range(1, g.near_size)
        ]

    def start(self):
        for copy in self.scatter():
            copy.start()

    def middle(self):
        g = self.groups
        for copy in self.scatter():
            copy.wait()
        total = self.pack[pl.ds(g.near * self.size, self.size)].astype(f32)
        for s in range(1, g.near_size):
            total = total + self.arrived[s - 1].astype(f32)
        self.crossed[g.far] = total.astype(self.crossed.dtype)
        for copy in self.cross():
            copy.start()

    def last(self):
        g = self.groups
        for copy in self.cross():
            copy.wait()
        total = self.crossed[0].astype(f32)
        for s in range(1, g.far_size):
            total = total + self.crossed[s].astype(f32)
        self.out[pl.ds(g.near * self.size, self.size)] = total.astype(self.out.dtype)
        for copy in self.gather():
            copy.start()

    def finish(self):
        for copy in self.gather():
            copy.wait()


def reduction_scratch(tiles, near_size, far_size, kind):
    size = tiles // near_size
    near = (near_size - 1,)
    far = (max(far_size - 1, 1),)
    dma = pltpu.SemaphoreType.DMA
    return [
        pltpu.VMEM((near_size - 1, size, TILE, LANES), kind),
        pltpu.VMEM((far_size, size, TILE, LANES), kind),
        dma(near),
        dma(near),
        dma(far),
        dma(far),
        dma(near),
        dma(near),
    ]


class Gather:
    def __init__(self, size, sources, targets, sems):
        self.size = size
        self.far = size // 2
        self.sources = sources
        self.targets = targets
        self.across_s, self.across_r, self.pair_s, self.pair_r, self.one_s, self.one_r, self.two_s, self.two_r = sems[:8]
        self.whole_s, self.whole_r, self.small_s, self.small_r, self.own = sems[8:]
        self.tensor = lax.axis_index("tensor")
        self.dp = lax.axis_index("dp")
        self.bit = self.dp % 2
        self.pair = {"dp": self.dp + 1 - 2 * self.bit, "tensor": self.tensor}
        self.near = self.tensor + 1 - 2 * (self.tensor % 2)
        self.core = {"dp": self.dp, "tensor": self.near}

    def device(self, step):
        return {"dp": self.dp, "tensor": (self.tensor + step) % self.size}

    def partners(self):
        return [self.device(s) for s in range(1, self.size)] + [self.pair]

    def slot(self, order):
        first = self.tensor if isinstance(order, int) and order % 2 == 0 else None
        if first is None:
            first = self.tensor + (order % 2) * (self.near - self.tensor)
        return (first + self.size - 2 * (order // 2)) % self.size

    def rows(self, which, part, bit):
        count = self.sources[which].shape[0] // 6
        return pl.ds((2 * part + bit) * count, count)

    def across(self, s, k):
        which, part = k // 3, k % 3
        rows = self.rows(which, part, self.bit)
        return remote(
            self.sources[which].at[rows, :],
            self.targets[which].at[self.tensor, rows, :],
            self.across_s.at[s - 1, k],
            self.across_r.at[s - 1, k],
            self.device(2 * s),
        )

    def onward(self, s, k, bit, sends, recvs, device):
        which, part = k // 3, k % 3
        rows = self.rows(which, part, bit)
        ref = self.targets[which].at[self.slot(2 * s), rows, :]
        return remote(ref, ref, sends.at[s - 1, k], recvs.at[s - 1, k], device)

    def swap(self, s, k):
        return self.onward(s, k, self.bit, self.pair_s, self.pair_r, self.pair)

    def share_one(self, s, k):
        return self.onward(s, k, self.bit, self.one_s, self.one_r, self.core)

    def share_two(self, s, k):
        return self.onward(s, k, 1 - self.bit, self.two_s, self.two_r, self.core)

    def whole(self, which):
        return remote(
            self.sources[which],
            self.targets[which].at[self.tensor],
            self.whole_s.at[which],
            self.whole_r.at[which],
            self.core,
        )

    def small(self, s, which):
        return remote(
            self.sources[which],
            self.targets[which].at[self.tensor],
            self.small_s.at[s - 1, which - 2],
            self.small_r.at[s - 1, which - 2],
            self.device(s),
        )

    def keep(self, which):
        return pltpu.make_async_copy(
            self.sources[which], self.targets[which].at[self.tensor], self.own.at[which]
        )

    def start(self):
        for which in range(4):
            self.keep(which).start()
        greet(self.partners())
        for k in range(6):
            for s in range(1, self.far):
                self.across(s, k).start()
        for which in range(2):
            self.whole(which).start()
        for s in range(1, self.size):
            for which in (2, 3):
                self.small(s, which).start()

    def forward_one(self, k):
        for s in range(1, self.far):
            self.across(s, k).wait_recv()
            self.swap(s, k).start()
            self.share_one(s, k).start()

    def forward_two(self, k):
        for s in range(1, self.far):
            self.swap(s, k).wait_recv()
            self.share_two(s, k).start()

    def arrive(self, order):
        if order == 0:
            for which in range(4):
                self.keep(which).wait()
            for s in range(1, self.size):
                for which in (2, 3):
                    self.small(s, which).wait()
        elif order == 1:
            for which in range(2):
                self.whole(which).wait()
        elif order % 2 == 1:
            for k in range(6):
                self.share_one(order // 2, k).wait_recv()
                self.share_two(order // 2, k).wait_recv()

    def finish(self):
        for s in range(1, self.far):
            for k in range(6):
                self.across(s, k).wait_send()
                self.swap(s, k).wait_send()
                self.share_one(s, k).wait_send()
                self.share_two(s, k).wait_send()


def norm_parts(values):
    center = values - jnp.mean(values, axis=-1, keepdims=True)
    root = lax.rsqrt(jnp.mean(center * center, axis=-1, keepdims=True) + norm_eps)
    return center * root, root


def norm_back(scaled, unit, root):
    return root * (
        scaled
        - jnp.mean(scaled, axis=-1, keepdims=True)
        - unit * jnp.mean(scaled * unit, axis=-1, keepdims=True)
    )


def feed_part(
    tokens,
    cotangent,
    cotangent_copy,
    out_weight,
    out_copy,
    left_s,
    right_s,
    scale_row,
    gain,
    shift,
    expand_left_t,
    expand_right,
    shrink_left_t,
    shrink_right,
    feed_scale,
    layer_out,
    grad_first_out,
    grad_context_out,
    pack,
    expand_s,
    shrink_s,
    x_s,
    normed_s,
    hidden_s,
    act_s,
    slope_s,
    branch_s,
    context_s,
    one_s,
    two_s,
    pre_s,
    gather,
):
    chunks = expand_s.shape[0]
    pieces = expand_s.shape[2] // LANES
    pack[...] = jnp.zeros_like(pack)

    def keep(first, values):
        for j in range(values.shape[1] // LANES):
            pack[first + j, :RANK, :] = values[:, j * LANES : (j + 1) * LANES]

    lam_one = feed_scale[0:1, :]
    lam_two = feed_scale[1:2, :]
    step = LANES
    steps = ROWS // step

    out_copy.wait()
    out_rank = dot_nt(context_s[...], left_s[...])
    out_low = (out_rank * scale_row).astype(bf16) * of_map(3)
    x_s[...] = dot_nn(context_s[...], out_weight[...]) + dot_nn(out_low, right_s[...])

    def first_norm(i, carry):
        rows = pl.ds(i * step, step)
        values = tokens[rows, :].astype(f32) + x_s[rows, :]
        x_s[rows, :] = values
        unit, root = norm_parts(values)
        normed = unit * gain[0:1, :] + shift[0:1, :]
        normed_s[rows, :] = normed
        hidden_s[rows, :] = normed.astype(bf16)
        return carry

    lax.fori_loop(0, steps, first_norm, 0)
    gather.forward_two(5)

    one_rank = dot_nt(hidden_s[...], expand_left_t[...])
    one_low = (one_rank * lam_one).astype(bf16)
    def expanded(order):
        gather.arrive(order)
        c = gather.slot(order)
        pre_s[order % 2] = dot_nn(hidden_s[...], expand_s[c]) + dot_nn(one_low, expand_right[c])

    two_rank = None
    expanded(0)
    for order in range(chunks):
        if order + 1 < chunks:
            expanded(order + 1)
        pre = pre_s[order % 2]
        cdf = 0.5 + 0.5 * lax.erf(pre * inverse_root_two)
        act_s[order] = (pre * cdf).astype(bf16)
        slope_s[order] = cdf + pre * jnp.exp(-0.5 * pre * pre) * inverse_root_tau
        c = gather.slot(order)
        part = dot_nn(act_s[order], shrink_s[c])
        branch_s[...] = part if order == 0 else branch_s[...] + part
        part = dot_nt(act_s[order], shrink_left_t[c])
        two_s[...] = part if order == 0 else two_s[...] + part
    two_rank = two_s[...]
    gather.finish()
    two_low = (two_rank * lam_two).astype(bf16)
    branch_s[...] += dot_nn(two_low, shrink_right[...])

    cotangent_copy.wait()

    def second_norm(i, carry):
        rows = pl.ds(i * step, step)
        unit, root = norm_parts(normed_s[rows, :] + branch_s[rows, :])
        layer_out[rows, :] = (unit * gain[1:2, :] + shift[1:2, :]).astype(bf16)
        grad = norm_back(cotangent[rows, :].astype(f32) * gain[1:2, :], unit, root)
        branch_s[rows, :] = grad
        return carry

    lax.fori_loop(0, steps, second_norm, 0)
    grad_branch = branch_s[...].astype(bf16)
    two_back = dot_nt(grad_branch, shrink_right[...])
    two_small = (two_back * lam_two).astype(bf16)
    two_small_t = two_small.T
    one_low_t = one_low.T
    keep(18, dot_tn(two_low, grad_branch))
    pack[24, 5:6, :RANK] = jnp.sum(two_rank * two_back, axis=0, keepdims=True)

    def shrunk(order):
        c = gather.slot(order)
        pre_s[order % 2] = dot_nt(grad_branch, shrink_s[c]) + dot_nn(two_small, shrink_left_t[c])

    shrunk(0)
    for order in range(chunks):
        if order + 1 < chunks:
            shrunk(order + 1)
        c = gather.slot(order)
        grad_pre = (pre_s[order % 2] * slope_s[order]).astype(bf16)
        keep(SPLIT_AT + (chunks + c) * pieces, dot_nn(two_small_t, act_s[order]))
        keep(SPLIT_AT + c * pieces, dot_nn(one_low_t, grad_pre))
        branch_s[...] += dot_nt(grad_pre, expand_s[c])
        part = dot_nt(grad_pre, expand_right[c])
        one_s[...] = part if order == 0 else one_s[...] + part
    one_back = one_s[...]
    one_small = (one_back * lam_one).astype(bf16)
    branch_s[...] += dot_nn(one_small, expand_left_t[...])
    keep(12, dot_tn(one_small, hidden_s[...]))
    pack[24, 4:5, :RANK] = jnp.sum(one_rank * one_back, axis=0, keepdims=True)

    def first_back(i, carry):
        rows = pl.ds(i * step, step)
        unit, root = norm_parts(x_s[rows, :])
        grad_first_out[rows, :] = norm_back(branch_s[rows, :] * gain[0:1, :], unit, root)
        return carry

    lax.fori_loop(0, steps, first_back, 0)
    grad_attended = grad_first_out[...].astype(bf16)
    out_back = dot_nt(grad_attended, right_s[...])
    out_small = (out_back * scale_row).astype(bf16) * of_map(3)
    grad_context = dot_nt(grad_attended, out_weight[...]) + dot_nn(out_small, left_s[...])
    for p in range(PAIRS):
        grad_context_out[p] = grad_context[:, p * LANES : (p + 1) * LANES].astype(bf16)
    keep(0, dot_tn(out_small, context_s[...])[3 * TILE : 3 * TILE + RANK, :])
    keep(6, dot_tn(out_low, grad_attended)[3 * TILE : 3 * TILE + RANK, :])
    pack[24, 3:4, :STACK] = jnp.sum(out_rank * out_back, axis=0, keepdims=True)


def front_kernel(
    segment,
    live,
    tokens,
    table,
    left_t,
    right,
    scale,
    gain,
    shift,
    expand_left_t,
    shrink_right,
    feed_scale,
    mix_weight,
    cotangent,
    out_weight,
    expand,
    shrink,
    expand_right,
    shrink_left_t,
    layer_out,
    grad_first,
    grad_context,
    pack,
    q_s,
    k_s,
    v_s,
    tq_s,
    tk_s,
    tr_s,
    left_s,
    right_s,
    rank_s,
    table_rank_s,
    shares_out,
    mix_s,
    cotangent_s,
    out_s,
    expand_s,
    shrink_s,
    expand_right_s,
    shrink_left_s,
    shares_s,
    bias_s,
    across_s,
    x_s,
    normed_s,
    hidden_s,
    act_s,
    slope_s,
    branch_s,
    context_s,
    one_s,
    two_s,
    pre_s,
    share_sems,
    load_sems,
    *gather_sems,
):
    mix_copies = [
        pltpu.make_async_copy(mix_weight.at[i], mix_s.at[i], load_sems.at[i]) for i in range(3)
    ]
    cotangent_copy = pltpu.make_async_copy(cotangent, cotangent_s, load_sems.at[3])
    out_copy = pltpu.make_async_copy(out_weight, out_s, load_sems.at[4])
    for copy in mix_copies:
        copy.start()
    gather = Gather(
        expand_s.shape[0],
        (expand, shrink, expand_right, shrink_left_t),
        (expand_s, shrink_s, expand_right_s, shrink_left_s),
        gather_sems,
    )
    gather.start()
    cotangent_copy.start()
    out_copy.start()
    left_s[...] = jnp.zeros_like(left_s)
    right_s[...] = jnp.zeros_like(right_s)
    for a in range(4):
        left_s[a * TILE : a * TILE + RANK, :] = left_t[:, a, :]
        right_s[a * TILE : a * TILE + RANK, :] = right[:, a, :]
    scale_row = spread(scale)
    attend_part(
        segment,
        live,
        tokens,
        table,
        mix_s,
        mix_copies,
        left_s,
        right_s,
        scale_row,
        rank_s,
        table_rank_s,
        shares_out,
        q_s,
        k_s,
        v_s,
        tq_s,
        tk_s,
        tr_s,
        context_s,
        shares_s,
        bias_s,
        across_s,
        share_sems,
        gather,
    )
    feed_part(
        tokens,
        cotangent_s,
        cotangent_copy,
        out_s,
        out_copy,
        left_s,
        right_s,
        scale_row,
        gain,
        shift,
        expand_left_t,
        expand_right_s,
        shrink_left_s,
        shrink_right,
        feed_scale,
        layer_out,
        grad_first,
        grad_context,
        pack,
        expand_s,
        shrink_s,
        x_s,
        normed_s,
        hidden_s,
        act_s,
        slope_s,
        branch_s,
        context_s,
        one_s,
        two_s,
        pre_s,
        gather,
    )

    def finish(p, carry):
        pltpu.make_async_copy(shares_s.at[p], shares_out.at[p], share_sems.at[p]).wait()
        return carry

    lax.fori_loop(0, PAIRS, finish, 0)


def front(size, tiles, *args):
    hidden = args[15].shape[1]
    piece = jax.ShapeDtypeStruct((PAIRS, ROWS, LANES), bf16)
    rows = jax.ShapeDtypeStruct((ROWS, WIDTH), bf16)
    dma = pltpu.SemaphoreType.DMA
    steps = (max(size // 2 - 1, 1), 6)
    return pl.pallas_call(
        front_kernel,
        out_shape=(
            rows,
            jax.ShapeDtypeStruct((ROWS, WIDTH), f32),
            piece,
            jax.ShapeDtypeStruct((tiles, TILE, LANES), f32),
            piece,
            piece,
            piece,
            piece,
            piece,
            rows,
            jax.ShapeDtypeStruct((STACK, WIDTH), bf16),
            jax.ShapeDtypeStruct((STACK, WIDTH), bf16),
            jax.ShapeDtypeStruct((ROWS, STACK), f32),
            jax.ShapeDtypeStruct((ROWS, STACK), f32),
            jax.ShapeDtypeStruct((PAIRS, 2, ROWS, ROWS), bf16),
        ),
        in_specs=[vmem()] * 12 + [anywhere()] * 7,
        out_specs=(vmem(),) * 14 + (anywhere(),),
        scratch_shapes=[
            pltpu.VMEM((3, WIDTH, WIDTH), bf16),
            pltpu.VMEM((ROWS, WIDTH), bf16),
            pltpu.VMEM((WIDTH, WIDTH), bf16),
            pltpu.VMEM((size, WIDTH, hidden), bf16),
            pltpu.VMEM((size, hidden, WIDTH), bf16),
            pltpu.VMEM((size, RANK, hidden), bf16),
            pltpu.VMEM((size, RANK, hidden), bf16),
            pltpu.VMEM((PAIRS, 2, ROWS, ROWS), bf16),
            pltpu.VMEM((ROWS, ROWS), f32),
            pltpu.VMEM((2, ROWS, ROWS), bf16),
            pltpu.VMEM((ROWS, WIDTH), f32),
            pltpu.VMEM((ROWS, WIDTH), f32),
            pltpu.VMEM((ROWS, WIDTH), bf16),
            pltpu.VMEM((size, ROWS, hidden), bf16),
            pltpu.VMEM((size, ROWS, hidden), f32),
            pltpu.VMEM((ROWS, WIDTH), f32),
            pltpu.VMEM((ROWS, WIDTH), bf16),
            pltpu.VMEM((ROWS, RANK), f32),
            pltpu.VMEM((ROWS, RANK), f32),
            pltpu.VMEM((2, ROWS, hidden), f32),
            dma((PAIRS,)),
            dma((5,)),
        ]
        + [dma(steps)] * 8
        + [dma((2,))] * 2
        + [dma((size - 1, 2))] * 2
        + [dma((4,))],
        compiler_params=pltpu.CompilerParams(
            vmem_limit_bytes=60 * 2**20, collective_id=0, has_side_effects=True
        ),
        name="front",
    )(*args)


def back_kernel(
    grad_context,
    q_s,
    k_s,
    v_s,
    tq_s,
    tk_s,
    left_s,
    right_s,
    rank_s,
    table_rank_s,
    scale,
    early,
    tokens_in,
    tr_in,
    mix_in,
    grad_first_in,
    shares_in,
    grad_tokens,
    early_out,
    tail_out,
    tokens,
    tr_s,
    mix_weight,
    grad_first,
    shares_s,
    gl_s,
    qf_s,
    kf_s,
    gq_s,
    gk_s,
    gt_s,
    grads_s,
    tables_s,
    tail,
    sems,
    load_sems,
    *reduce_refs,
):
    arrived, crossed = reduce_refs[0], reduce_refs[1]
    groups = Groups(arrived.shape[0] // 2 + 1, crossed.shape[0] * 2)
    first = Reduction(groups, early, arrived, crossed, early_out, reduce_refs[2:8])
    second = Reduction(groups, tail, reduce_refs[8], reduce_refs[9], tail_out, reduce_refs[10:16])
    row, lane = block_iotas()
    beyond = lane >= row
    inside = (row + lane <= LANES - 1).astype(bf16)
    ends = lax.broadcasted_iota(jnp.int32, (2 * LANES, LANES), 1)
    pick_first = (ends == 0).astype(bf16)
    pick_last = (ends == LANES - 1).astype(bf16)
    flip = (row + lane == LANES - 1).astype(bf16)

    def begin(p, carry):
        pltpu.make_async_copy(shares_in.at[p], shares_s.at[p], sems.at[p]).start()
        return carry

    lax.fori_loop(0, PAIRS, begin, 0)
    loads = [
        pltpu.make_async_copy(source, target, load_sems.at[i])
        for i, (source, target) in enumerate(
            (
                (tokens_in, tokens),
                (tr_in, tr_s),
                (mix_in, mix_weight),
                (grad_first_in, grad_first),
            )
        )
    ]
    greet(groups.partners())
    first.start()
    for copy in loads:
        copy.start()
    tail[...] = jnp.zeros_like(tail)
    scale_row = spread(scale)
    low = (rank_s[...] * scale_row).astype(bf16)
    table_low = (table_rank_s[...] * scale_row).astype(bf16)

    def keep(index, values):
        for j in range(values.shape[1] // LANES):
            tail[index + j] = values[:, j * LANES : (j + 1) * LANES].astype(bf16)

    def flipped(values):
        return jnp.concatenate(
            [
                dot_nn(flip, values[b * LANES : (b + 1) * LANES, :]).astype(bf16)
                for b in range(BLOCKS)
            ],
            axis=0,
        )

    def rows_of(group):
        return [
            slice(a * LANES, (a + 1) * LANES)
            for a in range(group * BACK_GROUP, (group + 1) * BACK_GROUP)
        ]

    def grads(p, which, group):
        rows = rows_of(group)
        every = slice(rows[0].start, rows[-1].stop)
        grad = dot_nt(grad_context[p, every, :] * head_mask(which), v_s[p])
        shares = [shares_s[p, which, r, :].astype(f32) for r in rows]
        prods = [
            grad[i * LANES : (i + 1) * LANES, :] * shares[i] for i in range(BACK_GROUP)
        ]
        inner = [jnp.sum(prod, axis=1, keepdims=True) for prod in prods]
        for i, r in enumerate(rows):
            gl_s[which, r, :] = (prods[i] - shares[i] * inner[i]).astype(bf16)

    def fold(which, group, target, turn):
        rows = rows_of(group)
        turned = [
            dot_nt(flip, gl_s[which, :, r]) if turn else dot_nn(flip, gl_s[which, r, :])
            for r in rows
        ]
        for t, r in zip(turned, rows):
            target[which, r, :ROWS] = t.astype(bf16)
        for i, r in enumerate(rows):
            target[which, r, ROWS:] = fold_rows(
                turned[i], group * BACK_GROUP + i, beyond, inside, pick_first, pick_last
            ).astype(bf16)

    def close(p, which, parts):
        gc_t, k_t, q_t, tk_t, tq_t, q_rev_t, k_rev_t = parts
        half = slice(which * 64, which * 64 + 64)
        gq_t = dot_nt(jnp.concatenate([k_t[half, :], tk_t[half, :]], axis=1), qf_s[which])
        gk_t = dot_nt(jnp.concatenate([q_t[half, :], tq_t[half, :]], axis=1), kf_s[which])
        gq_s[half, :] = (gq_t * score_scale).astype(bf16)
        gk_s[half, :] = (gk_t * score_scale).astype(bf16)
        gtk = dot_nn(q_rev_t[half, :], qf_s[which, :, ROWS:])
        gtq = dot_nn(k_rev_t[half, :], kf_s[which, :, ROWS:])
        gt_s[0, half, :] = (gtq * score_scale).astype(bf16)
        gt_s[1, half, :] = (gtk * score_scale).astype(bf16)
        gt_s[2, half, :] = dot_nn(gc_t[half, :], shares_s[p, which]).astype(bf16)

    sections = BLOCKS // BACK_GROUP
    pltpu.make_async_copy(shares_in.at[0], shares_s.at[0], sems.at[0]).wait()
    for group in range(sections):
        grads(0, 0, group)

    def pair(p, carry):
        later = jnp.minimum(p + 1, PAIRS - 1)

        @pl.when(p < PAIRS - 1)
        def _():
            pltpu.make_async_copy(
                shares_in.at[later], shares_s.at[later], sems.at[later]
            ).wait()

        @pl.when(p == 2)
        def _():
            first.middle()

        @pl.when(p == 4)
        def _():
            first.last()

        parts = (
            grad_context[p].T,
            k_s[p].T,
            q_s[p].T,
            tk_s[p].T,
            tq_s[p].T,
            flipped(q_s[p]).T,
            flipped(k_s[p]).T,
        )
        for group in range(sections):
            fold(0, group, qf_s, False)
            grads(p, 1, group)
            fold(0, group, kf_s, True)
        close(p, 0, parts)
        for group in range(sections):
            fold(1, group, qf_s, False)
            grads(later, 0, group)
            fold(1, group, kf_s, True)
        close(p, 1, parts)
        lanes = pl.ds(pl.multiple_of(p * LANES, LANES), LANES)
        for b in range(BLOCKS):
            rows = slice(b * LANES, (b + 1) * LANES)
            grads_s[0, rows, lanes] = dot_nt(flip, gq_s[:, rows]).astype(bf16)
            grads_s[1, rows, lanes] = dot_nt(flip, gk_s[:, rows]).astype(bf16)
        grads_s[2, :, lanes] = gt_s[2].T
        tables_s[0, :, lanes] = gt_s[0].T
        tables_s[1, :, lanes] = gt_s[1].T
        return carry

    lax.fori_loop(0, PAIRS, pair, 0)

    for copy in loads:
        copy.wait()

    def backs(source, count):
        total = None
        lane = lax.broadcasted_iota(jnp.int32, (1, STACK), 1)
        for which in range(count):
            part = dot_nt(source[which], right_s[...])
            part = jnp.where(lane // TILE == which, part, 0.0)
            total = part if total is None else total + part
        return total

    back = backs(grads_s, 3)
    table_back = backs(tables_s, 2)
    small = (back * scale_row).astype(bf16)
    table_small = (table_back * scale_row).astype(bf16)
    left_sum = dot_tn(small, tokens[...]) + dot_tn(table_small, tr_s[...])
    low_t = low.T
    table_low_t = table_low.T
    for which in range(3):
        rows = slice(which * TILE, (which + 1) * TILE)
        right_sum = dot_nn(low_t[rows, :], grads_s[which])
        if which < 2:
            right_sum = right_sum + dot_nn(table_low_t[rows, :], tables_s[which])
        keep(which * 6, left_sum[rows, :])
        keep(18 + which * 6, right_sum)
    tail[36, :1, :STACK] = jnp.sum(
        rank_s[...] * back + table_rank_s[...] * table_back, axis=0, keepdims=True
    ).astype(bf16)
    first.finish()
    second.start()
    grad_tokens[...] = grad_first[...] + dot_nn(small, left_s[...])
    grad_tokens[...] += dot_nt(grads_s[0], mix_weight[0])
    second.middle()
    grad_tokens[...] += dot_nt(grads_s[1], mix_weight[1])
    second.last()
    grad_tokens[...] += dot_nt(grads_s[2], mix_weight[2])
    second.finish()


def back(tail_tiles, near_size, far_size, *args):
    early = args[11]
    return pl.pallas_call(
        back_kernel,
        out_shape=(
            jax.ShapeDtypeStruct((ROWS, WIDTH), f32),
            jax.ShapeDtypeStruct(early.shape, f32),
            jax.ShapeDtypeStruct((tail_tiles, TILE, LANES), bf16),
        ),
        in_specs=[vmem()] * 12 + [anywhere()] * 5,
        out_specs=(vmem(),) * 3,
        scratch_shapes=[
            pltpu.VMEM((ROWS, WIDTH), bf16),
            pltpu.VMEM((ROWS, WIDTH), bf16),
            pltpu.VMEM((3, WIDTH, WIDTH), bf16),
            pltpu.VMEM((ROWS, WIDTH), f32),
            pltpu.VMEM((PAIRS, 2, ROWS, ROWS), bf16),
            pltpu.VMEM((2, ROWS, ROWS), bf16),
            pltpu.VMEM((2, ROWS, 2 * ROWS), bf16),
            pltpu.VMEM((2, ROWS, 2 * ROWS), bf16),
            pltpu.VMEM((LANES, ROWS), bf16),
            pltpu.VMEM((LANES, ROWS), bf16),
            pltpu.VMEM((3, LANES, ROWS), bf16),
            pltpu.VMEM((3, ROWS, WIDTH), bf16),
            pltpu.VMEM((2, ROWS, WIDTH), bf16),
            pltpu.VMEM((tail_tiles, TILE, LANES), bf16),
            pltpu.SemaphoreType.DMA((PAIRS,)),
            pltpu.SemaphoreType.DMA((4,)),
        ]
        + reduction_scratch(early.shape[0], near_size, far_size, f32)
        + reduction_scratch(tail_tiles, near_size, far_size, bf16),
        compiler_params=pltpu.CompilerParams(
            vmem_limit_bytes=58 * 2**20, collective_id=1, has_side_effects=True
        ),
        name="back",
    )(*args)


def unpack_kernel(
    early,
    tail,
    tokens_in,
    tokens_out,
    left,
    scale,
    right,
    expand_left_t,
    expand_right,
    shrink_left_t,
    feed_scale,
    shrink_right,
    sem,
):
    copy = pltpu.make_async_copy(tokens_in, tokens_out, sem)
    copy.start()
    me = lax.axis_index("tensor")
    pieces = expand_right.shape[1] // LANES
    split = SPLIT_AT + me * pieces
    skip = (early.shape[0] - SPLIT_AT) // 2
    for j in range(WIDTH // LANES):
        lanes = slice(j * LANES, (j + 1) * LANES)
        for which in range(3):
            left[:, which, lanes] = tail[which * 6 + j, :RANK, :].astype(f32)
            right[:, which, lanes] = tail[18 + which * 6 + j, :RANK, :].astype(f32)
        left[:, 3, lanes] = early[j, :RANK, :]
        right[:, 3, lanes] = early[6 + j, :RANK, :]
        expand_left_t[:, lanes] = early[12 + j, :RANK, :]
        shrink_right[:, lanes] = early[18 + j, :RANK, :]
    total = lax.axis_size("tensor") * pieces
    for j in range(pieces):
        lanes = slice(j * LANES, (j + 1) * LANES)
        expand_right[:, lanes] = early[split + j, :RANK, :]
        shrink_left_t[:, lanes] = early[split + total + j, :RANK, :]
    mixed = tail[36].astype(f32)
    for which in range(3):
        scale[which : which + 1, :] = mixed[:1, which * TILE : which * TILE + RANK]
    other = early[24]
    scale[3:4, :] = other[3:4, 3 * TILE : 3 * TILE + RANK]
    feed_scale[...] = other[4:6, :RANK]
    copy.wait()


def unpack(hidden, early, tail, tokens):
    mats = jax.ShapeDtypeStruct((RANK, 4, WIDTH), f32)
    small = jax.ShapeDtypeStruct((RANK, WIDTH), f32)
    split = jax.ShapeDtypeStruct((RANK, hidden), f32)
    return pl.pallas_call(
        unpack_kernel,
        out_shape=(
            jax.ShapeDtypeStruct((ROWS, WIDTH), f32),
            mats,
            jax.ShapeDtypeStruct((4, RANK), f32),
            mats,
            small,
            split,
            split,
            jax.ShapeDtypeStruct((2, RANK), f32),
            small,
        ),
        in_specs=[vmem(), vmem(), vmem()],
        out_specs=(anywhere(),) + (vmem(),) * 8,
        scratch_shapes=[pltpu.SemaphoreType.DMA],
        name="unpack",
    )(early, tail, tokens)


def body(
    tokens,
    segment,
    live,
    mix_weight,
    out_weight,
    position_table,
    norm_gain,
    norm_bias,
    mix_left,
    mix_scale,
    mix_right,
    expand_weight,
    expand_left,
    expand_right,
    shrink_weight,
    shrink_left,
    feed_scale,
    shrink_right,
    cotangent,
):
    tensor_size = lax.axis_size("tensor")
    near_size = tensor_size * 2
    far_size = lax.axis_size("dp") // 2
    hidden = expand_weight.shape[1]
    early_tiles = -(-(SPLIT_AT + 2 * tensor_size * hidden // LANES) // near_size) * near_size
    tail_tiles = -(-37 // near_size) * near_size
    left_t = jnp.transpose(mix_left, (2, 0, 1))
    right = jnp.transpose(mix_right, (1, 0, 2))
    layer_out, grad_first, grad_context, early, q, k, v, tq, tk, tr, *adapters, shares = front(
        tensor_size,
        early_tiles,
        segment.reshape(1, ROWS),
        live.reshape(1, ROWS),
        tokens,
        position_table,
        left_t,
        right,
        mix_scale,
        norm_gain,
        norm_bias,
        expand_left.T,
        shrink_right,
        feed_scale,
        mix_weight,
        cotangent,
        out_weight,
        expand_weight,
        shrink_weight,
        expand_right,
        shrink_left.T,
    )
    grad_tokens, early, tail = back(
        tail_tiles,
        near_size,
        far_size,
        grad_context,
        q,
        k,
        v,
        tq,
        tk,
        *adapters,
        mix_scale,
        early,
        tokens,
        tr,
        mix_weight,
        grad_first,
        shares,
    )
    grad_tokens, left, scale, right, expand_left, expand_right, shrink_left, feed_scale, shrink_right = unpack(
        hidden, early, tail, grad_tokens
    )
    return (
        layer_out,
        grad_tokens,
        jnp.transpose(left, (1, 2, 0)),
        scale,
        jnp.transpose(right, (1, 0, 2)),
        expand_left.T,
        expand_right,
        shrink_left.T,
        feed_scale,
        shrink_right,
    )


def solution(mesh):
    rows = P(("dp", "tensor"), None)
    line = P(("dp", "tensor"))
    return jax.shard_map(
        body,
        mesh=mesh,
        in_specs=(
            rows,
            line,
            line,
            P(),
            P(),
            P(),
            P(),
            P(),
            P(),
            P(),
            P(),
            P(None, "tensor"),
            P(),
            P(None, "tensor"),
            P("tensor", None),
            P("tensor", None),
            P(),
            P(),
            rows,
        ),
        out_specs=(
            rows,
            rows,
            P(),
            P(),
            P(),
            P(),
            P(None, "tensor"),
            P("tensor", None),
            P(),
            P(),
        ),
        check_vma=False,
    )
```

time: 146 us -> 119 us (0.82)
  Pallas kernels: 145 us -> 117 us
    pallas_call x1, Pallas kernels: 63.2 us -> 47 us  [back(): pl.pallas_call(back_kernel, out_shape=(jax.ShapeDtypeStruct((ROWS, WIDTH)...]
    pallas_call x2 -> x1, Pallas kernels: 78.5 us -> 66.5 us  [front(): pl.pallas_call(front_kernel, out_shape=(rows, jax.ShapeDtypeStruct((ROWS,...]
where the time goes in v3:
time: 119 us
  Pallas kernels  117 us (98%)
    pallas_call x1, Pallas kernels, front(): pl.pallas_call(front_kernel, out_shape=(rows, jax.ShapeDtypeStruct((ROWS,...  66.5 us
    pallas_call x1, Pallas kernels, back(): pl.pallas_call(back_kernel, out_shape=(jax.ShapeDtypeStruct((ROWS, WIDTH)...  47 us
    pallas_call x1, Pallas kernels, unpack(): pl.pallas_call(unpack_kernel, out_shape=(jax.ShapeDtypeStruct((ROWS, WIDT...  3.69 us

profile of v3, /device:TPU:0, one launch (start us, length us, event | category | flops | bytes accessed | tf_op | source)
XLA Modules:
  0.0 118.8 jit_solution(16980660217833842536)
XLA Ops:
  0.6 66.5 %front.1 = (bf16[512,768]{1,0:T(8,128)(2,1)}, f32[512,768]{1,0:T(8,128)}, bf16[6,512,128]{2,1,0:T(8,128)(2,1)}, f32[80,16,128]{2,1,0:T(8,128)}, bf16[6,512,128]{...) custom-call(s32[1,512]{1,0:T(1,128)} %bitcast.14, ...), custom_call_target="tpu_custom_call" | custom-call | tf_op jit(solution)/shard_map/front/pallas_call | solution.py:903
  67.2 47.0 %back.1 = (f32[512,768]{1,0:T(8,128)}, f32[80,16,128]{2,1,0:T(8,128)}, bf16[40,16,128]{2,1,0:T(8,128)(2,1)}) custom-call(bf16[6,512,128]{2,1,0:T(8,128)(2,1)} %get-tuple-element.38.grad_context, bf16[6,512,128]{2,1,0:T(8,128)(2,1)} %get-tuple-element.39.q_s, bf16[6,512,128]{2,1,0:T(8,128)(2,1)} %get-tuple-element.40.k_s, ...), custom_call_target="tpu_custom_call" | custom-call | tf_op jit(solution)/shard_map/back/pallas_call | solution.py:1187
  114.2 0.0 copy-start
  114.2 3.7 %unpack.1 = (f32[512,768]{1,0:T(8,128)}, f32[12,4,768]{2,1,0:T(4,128)}, f32[4,12]{1,0:T(4,128)}, f32[12,4,768]{2,1,0:T(4,128)}, f32[12,768]{1,0:T(8,128)}, /*ind...) custom-call(f32[80,16,128]{2,1,0:T(8,128)} %get-tuple-element.52.early, ...), custom_call_target="tpu_custom_call" | custom-call | tf_op jit(solution)/shard_map/unpack/pallas_call | solution.py:1271
  117.9 0.0 copy-done
  117.9 0.9 copy.30
Async XLA Ops:
  114.2 3.7 %copy-start = (bf16[512,768]{1,0:T(8,128)(2,1)S(1)}, bf16[512,768]{1,0:T(8,128)(2,1)}, u32[]{:S(2)}) copy-start(bf16[512,768]{1,0:T(8,128)(2,1)} %get-tuple-element.74) | copy-start | bytes 2359300
